TPU v7x, 32 devices: a whole 2x2x4 slice. The times are simulated.
32 devices in a mesh: groups: 2 (over y), train: 4 (over z), test: 2 (over x), proj: 2 (over core).
Axes of the slice: x: 2, y: 2, z: 4, core: 2. Of those that a mesh axis runs over, the one named last changes fastest.
Arguments:
- train_acts: bfloat16 [16, 128, 4096], P(('groups', 'train', 'test'), None, 'proj'), parts along dimension 0, may hold values from -6 to 6
- train_grads: bfloat16 [16, 128, 14336], P(('groups', 'train', 'test'), None, 'proj'), parts along dimension 0, may hold values from -6 to 6
- train_segs: int32 [16, 128], P(('groups', 'train', 'test')), parts along dimension 0, may hold values from 0 to 7, never falling along the last dimension, each value on 1 to 24 neighbouring positions
- train_mask: int32 [16, 128], P(('groups', 'train', 'test')), parts along dimension 0, may hold values 0 or 1
- test_acts: bfloat16 [16, 64, 4096], P(('groups', 'train', 'test'), None, 'proj'), parts along dimension 0, may hold values from -6 to 6
- test_grads: bfloat16 [16, 64, 14336], P(('groups', 'train', 'test'), None, 'proj'), parts along dimension 0, may hold values from -6 to 6
- test_segs: int32 [16, 64], P(('groups', 'train', 'test')), parts along dimension 0, may hold values from 0 to 3, never falling along the last dimension, each value on 1 to 24 neighbouring positions
- test_mask: int32 [16, 64], P(('groups', 'train', 'test')), parts along dimension 0, may hold values 0 or 1
- proj_in: bfloat16 [4096, 32], P('proj'), may hold values from -0.09375 to 0.09375
- proj_out: bfloat16 [14336, 32], P('proj'), may hold values from -0.046875 to 0.046875
Outputs:
- scores: float32 [128, 32], P(('groups', 'train', 'test'), 'proj'), parts along dimension 0
There are 2 independent parts, one for each index of `groups`. A program takes and returns all parts, laid end to end along the dimension named above; an argument that names none is the same for every part. Nothing has to cross between parts.
Inputs may be any that keep to these rules, and one draw needn't show every extreme that they name: `train_segs`: within each shard's row the example numbers never fall and every number 0 to 7 names 1 to 24 tokens. `test_segs`: within each shard's row the example numbers never fall and every number 0 to 3 names 1 to 24 tokens.
All inputs are finite; a program needn't handle non-finite values. No bound on the sum of `train_mask` or of `test_mask` on one device may be relied on, other than what follows from the above.
Results may differ from a plain program's by a relative error of at most 0.0003.
Values sent between devices are 32-bit elements; how exact they have to be, the bound alone decides.
No kernel may reach another device: no remote copies, remote signals or barrier semaphores. Data moves between devices by JAX's collectives and lax.ppermute only.
A program may use at most 64 MiB of HBM per device.

v0:
```python
import jax
import jax.numpy as jnp
from jax import lax
from jax.sharding import PartitionSpec as P

EX_DEV = 8
TEX_DEV = 4


def per_example(xp, gp, segs, mask, count):
    xp = xp * mask.reshape(-1, 1).astype(jnp.float32)
    outer = (xp[:, :, None] * gp[:, None, :]).reshape(xp.shape[0], -1)
    onehot = (jnp.arange(count, dtype=jnp.int32)[:, None] == segs).astype(jnp.float32)
    return jnp.dot(onehot, outer, precision=lax.Precision.HIGHEST)


def body(
    train_acts,
    train_grads,
    train_segs,
    train_mask,
    test_acts,
    test_grads,
    test_segs,
    test_mask,
    proj_in,
    proj_out,
):

    def project(acts, grads):
        rows = acts.shape[0] * acts.shape[1]
        xp = jnp.dot(acts.reshape(rows, -1), proj_in, preferred_element_type=jnp.float32)
        gp = jnp.dot(grads.reshape(rows, -1), proj_out, preferred_element_type=jnp.float32)
        return (xp, gp)

    train_xp, train_gp = project(train_acts, train_grads)
    test_xp, test_gp = project(test_acts, test_grads)
    train_xp, train_gp, test_xp, test_gp = lax.psum((train_xp, train_gp, test_xp, test_gp), "proj")
    train_full = per_example(train_xp, train_gp, train_segs, train_mask, EX_DEV)
    test_full = per_example(test_xp, test_gp, test_segs, test_mask, TEX_DEV)
    width = train_full.shape[1]
    nproj = lax.axis_size("proj")
    groups = lax.axis_size(("train", "test"))
    half = width // nproj
    offset = lax.axis_index("proj") * half
    train_half = lax.dynamic_slice_in_dim(train_full, offset, half, 1)
    total_ex = EX_DEV * groups
    partial_rows = jnp.dot(train_half.T, train_full, precision=lax.Precision.HIGHEST)
    summed = lax.psum(partial_rows, ("train", "test"))
    gram = lax.all_gather(summed, "proj", axis=0, tiled=True)
    hessian = gram / total_ex + jnp.eye(width, dtype=jnp.float32)
    factor = jnp.linalg.cholesky(hessian)
    solved = jax.scipy.linalg.cho_solve((factor, True), test_full.T)
    sent = lax.dynamic_slice_in_dim(solved, offset, half, 0).T
    scale = 1.0 / jnp.sqrt(jnp.float32(width))
    partial_scores = (
        jnp.dot(
            train_half,
            lax.all_gather(sent, ("train", "test"), axis=0, tiled=True).T,
            precision=lax.Precision.HIGHEST,
        )
        * scale
    )
    return lax.psum_scatter(partial_scores, "proj", scatter_dimension=1, tiled=True)


def solution(mesh):
    return jax.shard_map(
        body,
        mesh=mesh,
        in_specs=(
            P(("groups", "train", "test"), None, "proj"),
            P(("groups", "train", "test"), None, "proj"),
            P(("groups", "train", "test"), None),
            P(("groups", "train", "test"), None),
            P(("groups", "train", "test"), None, "proj"),
            P(("groups", "train", "test"), None, "proj"),
            P(("groups", "train", "test"), None),
            P(("groups", "train", "test"), None),
            P("proj", None),
            P("proj", None),
        ),
        out_specs=P(("groups", "train", "test"), "proj"),
        check_vma=False,
    )
```

profile of v0, /device:TPU:0, one launch (start us, length us, event | category | flops | bytes accessed | tf_op | source)
XLA Modules:
  0.0 536.2 jit_solution(18331514094432615925)
XLA Ops:
  8.0 1.7 fusion.1
  9.7 1.7 fusion.6
  13.1 3.9 all-reduce.1
  17.4 3.2 fusion.66
  20.7 104.3 %all-reduce.4.cloned.1.call-done = f32[512,1024]{0,1:T(8,128)} async-done(((f32[512,1024]{0,1:T(8,128)}), f32[512,1024]{0,1:T(8,128)}) %all-reduce.4.cloned.1.call-update) | async-done | bytes 2097168 | tf_op jit(solution)/shard_map/psum | solution.py:49
  125.6 14.4 %all-gather.3.cloned.1.call-done = f32[1024,1024]{0,1:T(8,128)} async-done(((f32[512,1024]{0,1:T(8,128)}), f32[1024,1024]{0,1:T(8,128)}) %all-gather.3.cloned.1.call-update) | async-done | bytes 4194320 | tf_op jit(solution)/shard_map/all_gather | solution.py:50
  140.0 5.0 convert_add_fusion
  145.0 5.6 %copy.20 = f32[1024,1024]{1,0:T(8,128)} copy(f32[1024,1024]{0,1:T(8,128)} %convert_add_fusion) | data formatting | bytes 8388608 | tf_op jit(solution)/shard_map/add | solution.py:51
  150.6 4.5 fusion
  155.1 1.9 copy-done.1
  157.0 11.7 %cholesky.223 = f32[128,128]{1,0:T(8,128)S(1)} custom-call(f32[128,128]{1,0:T(8,128)S(1)} %cholesky.580), custom_call_target="Cholesky" | custom-call | tf_op jit(solution)/shard_map/jit(cholesky)/cholesky | solution.py:52
  168.8 2.5 cholesky.255
  171.3 9.8 %custom-call.66 = f32[1,128,128]{1,2,0:T(8,128)S(1)} custom-call(f32[1,128,128]{2,1,0:T(8,128)S(1)} %get-tuple-element.48), custom_call_target="InvertDiagBlocksLowerTriangular" | custom-call | tf_op jit(solution)/shard_map/jit(cholesky)/cholesky | solution.py:52
  181.1 2.4 constant_dynamic-update-slice_fusion.49
  183.5 1.5 convolution_subtract_fusion
  185.0 12.2 %cholesky.244 = f32[128,128]{1,0:T(8,128)S(1)} custom-call(f32[128,128]{1,0:T(8,128)S(1)} %cholesky.584), custom_call_target="Cholesky" | custom-call | tf_op jit(solution)/shard_map/jit(cholesky)/cholesky | solution.py:52
  197.9 9.8 %custom-call.67 = f32[1,128,128]{1,2,0:T(8,128)S(1)} custom-call(f32[1,128,128]{2,1,0:T(8,128)S(1)} %get-tuple-element.45), custom_call_target="InvertDiagBlocksLowerTriangular" | custom-call | tf_op jit(solution)/shard_map/jit(cholesky)/cholesky | solution.py:52
  208.9 2.1 convolution_subtract_fusion.1
  211.0 11.7 %cholesky.468 = f32[128,128]{1,0:T(8,128)S(1)} custom-call(f32[128,128]{1,0:T(8,128)S(1)} %cholesky.589), custom_call_target="Cholesky" | custom-call | tf_op jit(solution)/shard_map/jit(cholesky)/cholesky | solution.py:52
  223.4 9.8 %custom-call.68 = f32[1,128,128]{1,2,0:T(8,128)S(1)} custom-call(f32[1,128,128]{2,1,0:T(8,128)S(1)} %get-tuple-element.42), custom_call_target="InvertDiagBlocksLowerTriangular" | custom-call | tf_op jit(solution)/shard_map/jit(cholesky)/cholesky | solution.py:52
  234.4 2.3 convolution_subtract_fusion.2
  236.7 11.9 %cholesky.487 = f32[128,128]{1,0:T(8,128)S(1)} custom-call(f32[128,128]{1,0:T(8,128)S(1)} %cholesky.594), custom_call_target="Cholesky" | custom-call | tf_op jit(solution)/shard_map/jit(cholesky)/cholesky | solution.py:52
  249.2 9.8 %custom-call.69 = f32[1,128,128]{1,2,0:T(8,128)S(1)} custom-call(f32[1,128,128]{2,1,0:T(8,128)S(1)} %get-tuple-element.39), custom_call_target="InvertDiagBlocksLowerTriangular" | custom-call | tf_op jit(solution)/shard_map/jit(cholesky)/cholesky | solution.py:52
  260.2 2.3 convolution_subtract_fusion.3
  262.5 11.7 %cholesky.506 = f32[128,128]{1,0:T(8,128)S(1)} custom-call(f32[128,128]{1,0:T(8,128)S(1)} %cholesky.599), custom_call_target="Cholesky" | custom-call | tf_op jit(solution)/shard_map/jit(cholesky)/cholesky | solution.py:52
  274.9 10.0 %custom-call.70 = f32[1,128,128]{1,2,0:T(8,128)S(1)} custom-call(f32[1,128,128]{2,1,0:T(8,128)S(1)} %get-tuple-element.36), custom_call_target="InvertDiagBlocksLowerTriangular" | custom-call | tf_op jit(solution)/shard_map/jit(cholesky)/cholesky | solution.py:52
  285.9 2.3 convolution_subtract_fusion.4
  288.2 11.7 %cholesky.526 = f32[128,128]{1,0:T(8,128)S(1)} custom-call(f32[128,128]{1,0:T(8,128)S(1)} %cholesky.604), custom_call_target="Cholesky" | custom-call | tf_op jit(solution)/shard_map/jit(cholesky)/cholesky | solution.py:52
  300.5 9.8 %custom-call.71 = f32[1,128,128]{1,2,0:T(8,128)S(1)} custom-call(f32[1,128,128]{2,1,0:T(8,128)S(1)} %get-tuple-element.33), custom_call_target="InvertDiagBlocksLowerTriangular" | custom-call | tf_op jit(solution)/shard_map/jit(cholesky)/cholesky | solution.py:52
  311.3 2.0 convolution_subtract_fusion.5
  313.3 12.1 %cholesky.546 = f32[128,128]{1,0:T(8,128)S(1)} custom-call(f32[128,128]{1,0:T(8,128)S(1)} %cholesky.609), custom_call_target="Cholesky" | custom-call | tf_op jit(solution)/shard_map/jit(cholesky)/cholesky | solution.py:52
  326.1 9.8 %custom-call.72 = f32[1,128,128]{1,2,0:T(8,128)S(1)} custom-call(f32[1,128,128]{2,1,0:T(8,128)S(1)} %get-tuple-element.30), custom_call_target="InvertDiagBlocksLowerTriangular" | custom-call | tf_op jit(solution)/shard_map/jit(cholesky)/cholesky | solution.py:52
  336.7 1.8 convolution_subtract_fusion.6
  338.5 11.7 %cholesky.564 = f32[128,128]{1,0:T(8,128)S(1)} custom-call(f32[128,128]{1,0:T(8,128)S(1)} %convolution_subtract_fusion.6), custom_call_target="Cholesky" | custom-call | tf_op jit(solution)/shard_map/jit(cholesky)/cholesky | solution.py:52
  360.6 4.8 select_select_fusion
  365.4 22.8 %while.1 = (s32[]{:T(128)}, f32[1024,1024]{1,0:T(8,128)}, s32[8,2]{0,1:T(2,128)S(1)}, f32[8,128,128]{2,1,0:T(8,128)S(1)}, s32[]{:T(128)}) while((s32[]{:T(128)}, f32[1024,1024]{1,0:T(8,128)}, s32[8,2]{0,1:T(2,128)S(1)}, f32[8,128,128]{2,1,0:T(8,128)S(1)}, s32[]{:T(128)}) %tuple.56), condition=%wide.while_cond, body=%wide.while_body.sunk | while | flops 2 | bytes 131189 | solution.py:53
  366.0 2.2 bitcast_dynamic-update-slice_fusion.2
  368.8 2.2 bitcast_dynamic-update-slice_fusion.2
  371.7 2.2 bitcast_dynamic-update-slice_fusion.2
  374.6 2.2 bitcast_dynamic-update-slice_fusion.2
  377.4 2.2 bitcast_dynamic-update-slice_fusion.2
  380.3 2.2 bitcast_dynamic-update-slice_fusion.2
  383.2 2.2 bitcast_dynamic-update-slice_fusion.2
  386.0 2.2 bitcast_dynamic-update-slice_fusion.2
  388.2 78.8 %custom-call.73 = f32[8,128,128]{1,2,0:T(8,128)S(1)} custom-call(f32[8,128,128]{2,1,0:T(8,128)S(1)} %get-tuple-element.12), custom_call_target="InvertDiagBlocksLowerTriangular" | custom-call | tf_op jit(solution)/shard_map/jit(_cho_solve)/triangular_solve | solution.py:53
  475.7 1.5 convolution_subtract_fusion.8
  488.0 30.8 %all-gather = f32[8,4,512]{2,1,0:T(4,128)S(1)} all-gather(f32[1,4,512]{2,1,0:T(4,128)S(1)} %dynamic-slice_bitcast_fusion), channel_id=1, replica_groups=mesh['groups'=2,'train'=4,'test'=2,'proj'=2] {'train','test'}, dimensions={0}, use_global_device_ids=true | all-gather | bytes 73728 | tf_op jit(solution)/shard_map/all_gather | solution.py:59
  519.7 8.4 %reduce-scatter.4.cloned.1.call-done = f32[16,8]{1,0:T(8,128)} async-done(((f32[32,8]{1,0:T(8,128)}), f32[16,8]{1,0:T(8,128)}) %reduce-scatter.4.cloned.1.call-update) | async-done | bytes 528
  (134 shorter events, 46.2 us)
Async XLA Ops:
  6.5 1.5 copy-start
  6.5 6.3 %copy-start.2 = (bf16[2048,32]{0,1:T(8,128)(2,1)S(1)}, bf16[2048,32]{0,1:T(8,128)(2,1)}, u32[]{:S(2)}) copy-start(bf16[2048,32]{0,1:T(8,128)(2,1)} %param.18) | copy-start | bytes 393220
  6.5 6.3 %copy-start.3 = (bf16[1,64,2048]{2,1,0:T(8,128)(2,1)S(1)}, bf16[1,64,2048]{2,1,0:T(8,128)(2,1)}, u32[]{:S(2)}) copy-start(bf16[1,64,2048]{2,1,0:T(8,128)(2,1)} %param.14) | copy-start | bytes 786436
  6.5 6.5 %copy-start.6 = (s32[1,128]{1,0:T(1,128)S(1)}, s32[1,128]{1,0:T(1,128)}, u32[]{:S(2)}) copy-start(s32[1,128]{1,0:T(1,128)} %param.13) | copy-start | bytes 1540
  6.5 10.5 %copy-start.4 = (s32[1,128]{1,0:T(1,128)S(1)}, s32[1,128]{1,0:T(1,128)}, u32[]{:S(2)}) copy-start(s32[1,128]{1,0:T(1,128)} %param.12) | copy-start | bytes 1540
  6.5 118.4 %all-reduce.4.cloned.1.call-start = ((), (), s32[]{:S(2)}) async-start(), calls=%async_computation.1 | async-start | bytes 4194304 | tf_op jit(solution)/shard_map/psum | solution.py:49
  11.4 113.7 %copy-start.7 = (s32[1,64]{1,0:T(1,128)S(1)}, s32[1,64]{1,0:T(1,128)}, u32[]{:S(2)}) copy-start(s32[1,64]{1,0:T(1,128)} %param.17) | copy-start | bytes 772
  12.8 112.4 %copy-start.5 = (s32[1,64]{1,0:T(1,128)S(1)}, s32[1,64]{1,0:T(1,128)}, u32[]{:S(2)}) copy-start(s32[1,64]{1,0:T(1,128)} %param.16) | copy-start | bytes 772
  20.6 119.4 %all-gather.3.cloned.1.call-start = ((), (), s32[]{:S(2)}) async-start(), calls=%async_computation.2 | async-start | bytes 6291456 | tf_op jit(solution)/shard_map/all_gather | solution.py:50
  125.0 403.1 %reduce-scatter.4.cloned.1.call-start = ((), (), s32[]{:S(2)}) async-start(), calls=%async_computation.3 | async-start | bytes 24576
  155.1 1.9 copy-start.1
Sparse Core Ops, SparseCore 0:
  20.7 104.2 all-reduce.3
  126.5 13.3 all-gather.2
  519.8 8.2 reduce-scatter.3
where the time goes:
time: 541 us; the launch traced here: 536 us
  other arithmetic  266 us (49%)
  waiting for transfers between devices  127 us (23%)
  matrix products  52.6 us (10%)
  local copies, waits for them, and re-layouts  36.6 us (7%)
  blocking collectives  34.7 us (6%)
  between operations  18.8 us (3%)
    another operation x30, other arithmetic, body(): factor = jnp.linalg.cholesky(hessian)  173 us
    psum x1, waiting for transfers between devices, body(): summed = lax.psum(partial_rows, ('train', 'test'))  104 us
    another operation x3, other arithmetic, body(): solved = jax.scipy.linalg.cho_solve((factor, True), test_full.T)  83.6 us
    all_gather x1, blocking collectives, body(): lax.all_gather(sent, ('train', 'test'), axis=0, tiled=True)  30.8 us
    another operation x14, matrix products, body(): factor = jnp.linalg.cholesky(hessian)  23.1 us
    another operation x24, local copies, waits for them, and re-layouts  22.7 us
    another operation x30, matrix products, body(): solved = jax.scipy.linalg.cho_solve((factor, True), test_full.T)  20.6 us
    all_gather x1, waiting for transfers between devices, body(): gram = lax.all_gather(summed, 'proj', axis=0, tiled=True)  14.4 us
  transfers between devices with their start and end apart: 3, of which 3 were waited for; matrix products, arithmetic and copies ran while one was open for 0% of the time, Pallas kernels for 0%

commit v1 on v0

--- a/solution.py
+++ b/solution.py
@@ -36,32 +36,25 @@
     train_xp, train_gp = project(train_acts, train_grads)
     test_xp, test_gp = project(test_acts, test_grads)
     train_xp, train_gp, test_xp, test_gp = lax.psum((train_xp, train_gp, test_xp, test_gp), "proj")
-    train_full = per_example(train_xp, train_gp, train_segs, train_mask, EX_DEV)
-    test_full = per_example(test_xp, test_gp, test_segs, test_mask, TEX_DEV)
-    width = train_full.shape[1]
-    nproj = lax.axis_size("proj")
-    groups = lax.axis_size(("train", "test"))
-    half = width // nproj
-    offset = lax.axis_index("proj") * half
-    train_half = lax.dynamic_slice_in_dim(train_full, offset, half, 1)
-    total_ex = EX_DEV * groups
-    partial_rows = jnp.dot(train_half.T, train_full, precision=lax.Precision.HIGHEST)
-    summed = lax.psum(partial_rows, ("train", "test"))
-    gram = lax.all_gather(summed, "proj", axis=0, tiled=True)
-    hessian = gram / total_ex + jnp.eye(width, dtype=jnp.float32)
-    factor = jnp.linalg.cholesky(hessian)
-    solved = jax.scipy.linalg.cho_solve((factor, True), test_full.T)
-    sent = lax.dynamic_slice_in_dim(solved, offset, half, 0).T
+    train_own = per_example(train_xp, train_gp, train_segs, train_mask, EX_DEV)
+    test_own = per_example(test_xp, test_gp, test_segs, test_mask, TEX_DEV)
+    width = train_own.shape[1]
+    shards = lax.axis_size(("train", "test"))
+    total_ex = EX_DEV * shards
+    total_tex = TEX_DEV * shards
+    both = lax.all_gather(jnp.concatenate([train_own, test_own], 0), ("train", "test"), axis=0)
+    train_full = both[:, :EX_DEV].reshape(total_ex, width)
+    test_full = both[:, EX_DEV:].reshape(total_tex, width)
+    cols = total_tex // lax.axis_size("proj")
+    test_half = lax.dynamic_slice_in_dim(test_full, lax.axis_index("proj") * cols, cols, 0)
+    gram = jnp.dot(train_full, train_full.T, precision=lax.Precision.HIGHEST)
+    cross = jnp.dot(train_full, test_half.T, precision=lax.Precision.HIGHEST)
+    system = gram / total_ex + jnp.eye(total_ex, dtype=jnp.float32)
+    factor = jnp.linalg.cholesky(system)
+    solved = jax.scipy.linalg.cho_solve((factor, True), cross)
     scale = 1.0 / jnp.sqrt(jnp.float32(width))
-    partial_scores = (
-        jnp.dot(
-            train_half,
-            lax.all_gather(sent, ("train", "test"), axis=0, tiled=True).T,
-            precision=lax.Precision.HIGHEST,
-        )
-        * scale
-    )
-    return lax.psum_scatter(partial_scores, "proj", scatter_dimension=1, tiled=True)
+    row = lax.axis_index(("train", "test")) * EX_DEV
+    return lax.dynamic_slice_in_dim(solved, row, EX_DEV, 0) * scale
 
 
 def solution(mesh):

time: 541 us -> 56.1 us (0.10)
  other arithmetic: 266 us -> 12.8 us
  waiting for transfers between devices: 127 us -> 0 us
  matrix products: 52.6 us -> 5.7 us
  local copies, waits for them, and re-layouts: 36.6 us -> 0.22 us
  between operations: 18.8 us -> 0.21 us
    another operation x33 -> x5, other arithmetic: 256 us -> 12.1 us  [the longest x3 6.52 us: body(): factor = jnp.linalg.cholesky(system)]
    psum x1 -> x0, waiting for transfers between devices: 104 us -> none  [body(): summed = lax.psum(partial_rows, ('train', 'test'))]
    another operation x44 -> x2, matrix products: 43.6 us -> 0.33 us  [body(): solved = jax.scipy.linalg.cho_solve((factor, True), cross)]
    another operation x37 -> x0, local copies, waits for them, and re-layouts: 25.3 us -> none
    all_gather x1 -> x0, waiting for transfers between devices: 14.4 us -> none  [body(): gram = lax.all_gather(summed, 'proj', axis=0, tiled=True)]
    unnamed x4 -> x0, waiting for transfers between devices: 8.44 us -> none
    unnamed x38 -> x16, local copies, waits for them, and re-layouts: 5.75 us -> 0.08 us
    add x1 -> x0, local copies, waits for them, and re-layouts: 5.61 us -> none  [body(): hessian = gram / total_ex + jnp.eye(width, dtype=jnp.float32)]
  transfers between devices with their start and end apart: 3 -> 0, of which waited for: 3 -> 0; matrix products, arithmetic and copies ran while one was open for 0% -> 0% of each run, Pallas kernels for 0% -> 0%
where the time goes in v1:
time: 56.1 us; the launch traced here: 55.9 us
  blocking collectives  36.9 us (66%)
  other arithmetic  12.8 us (23%)
  matrix products  5.7 us (10%)
    all_gather x1, blocking collectives, body(): lax.all_gather(jnp.concatenate([train_own, test_own], 0), ('train', 'test...  33 us
    another operation x3, other arithmetic, body(): factor = jnp.linalg.cholesky(system)  6.52 us
    another operation x2, other arithmetic, body(): solved = jax.scipy.linalg.cho_solve((factor, True), cross)  5.55 us
    psum x1, blocking collectives, body(): lax.psum((train_xp, train_gp, test_xp, test_gp), 'proj')  3.91 us
    dot_general x2, matrix products, project(): jnp.dot(grads.reshape(rows, -1), proj_out, preferred_element_type=jnp.flo...  2.51 us
    dot_general x2, matrix products, project(): jnp.dot(acts.reshape(rows, -1), proj_in, preferred_element_type=jnp.float32)  1.46 us

profile of v1, /device:TPU:0, one launch (start us, length us, event | category | flops | bytes accessed | tf_op | source)
XLA Modules:
  0.0 55.9 jit_solution(17503520398503189045)
XLA Ops:
  0.0 0.0 copy-start
  0.0 0.0 copy-start.1
  0.0 0.0 copy-start.3
  0.0 0.0 copy-start.2
  0.0 1.8 %fusion.2 = f32[64,32]{0,1:T(8,128)S(1)} fusion(bf16[7168,32]{0,1:T(8,128)(2,1)} %param.19, bf16[1,64,7168]{2,1,0:T(8,128)(2,1)} %param.15), kind=kOutput, calls=%fused_computation.3 | convolution fusion | flops 29360128 | bytes 1384448 | tf_op jit(solution)/shard_map/dot_general | solution.py:33
  1.8 0.0 copy-start.6
  1.8 1.2 %fusion.6 = f32[64,32]{0,1:T(8,128)S(1)} fusion(bf16[2048,32]{0,1:T(8,128)(2,1)} %param.18, bf16[1,64,2048]{2,1,0:T(8,128)(2,1)} %param.14), kind=kOutput, calls=%fused_computation.8 | convolution fusion | flops 8388608 | bytes 401408 | tf_op jit(solution)/shard_map/dot_general | solution.py:32
  3.0 0.0 copy-done
  3.0 0.0 copy-done.1
  3.0 0.0 copy-start.4
  3.1 0.0 copy-start.7
  3.1 0.0 copy-start.5
  3.1 0.7 %fusion = f32[128,32]{0,1:T(8,128)S(1)} fusion(bf16[7168,32]{0,1:T(8,128)(2,1)S(1)} %copy-done.1, bf16[1,128,7168]{2,1,0:T(8,128)(2,1)S(1)} %copy-done), kind=kOutput, calls=%fused_computation | convolution fusion | flops 58720256 | bytes 2310144 | tf_op jit(solution)/shard_map/dot_general | solution.py:33
  3.8 0.0 copy-done.3
  3.8 0.0 copy-done.2
  3.8 0.3 fusion.4
  4.1 3.9 %all-reduce = (f32[64,32]{0,1:T(8,128)S(1)}, f32[64,32]{0,1:T(8,128)S(1)}, f32[128,32]{0,1:T(8,128)S(1)}, f32[128,32]{0,1:T(8,128)S(1)}) all-reduce(f32[64,32]{0,1:T(8,128)S(1)} %fusion.2, f32[64,32]{0,1:T(8,128)S(1)} %fusion.6, f32[128,32]{0,1:T(8,128)S(1)} %fusion, ...), channel_id=1, replica_groups=mesh['groups'=2,'train'=4,'test'=2,'proj'=2] {'proj'}, use_global_device_ids=true, to_apply=%region_3.0 | all-reduce | flops 12288 | bytes 98304 | tf_op jit(solution)/shard_map/psum | solution.py:38
  8.0 0.0 copy-done.6
  8.0 0.1 broadcast_multiply_fusion
  8.1 0.0 copy-done.4
  8.1 0.4 fusion.19
  8.5 0.0 copy-done.7
  8.5 0.1 broadcast_multiply_fusion.1
  8.6 0.0 copy-done.5
  8.6 0.3 fusion.17
  9.0 33.0 %all-gather.1 = f32[8,12,1024]{2,1,0:T(8,128)S(1)} all-gather(f32[1,12,1024]{2,1,0:T(8,128)S(1)} %maximum_bitcast_fusion), channel_id=2, replica_groups=mesh['groups'=2,'train'=4,'test'=2,'proj'=2] {'train','test'}, dimensions={0}, use_global_device_ids=true | all-gather | bytes 442368 | tf_op jit(solution)/shard_map/all_gather | solution.py:45
  42.1 0.3 fusion.8
  42.3 0.4 convolution_multiply_fusion
  42.8 0.1 copy.20
  42.9 5.8 %cholesky.17 = f32[64,64]{1,0:T(8,128)S(1)} custom-call(f32[64,64]{1,0:T(8,128)S(1)} %fusion.16), custom_call_target="Cholesky" | custom-call | tf_op jit(solution)/shard_map/jit(cholesky)/cholesky | solution.py:53
  48.7 0.6 %compare_reduce_fusion = pred[]{:T(512)} fusion(f32[64]{0:T(128)S(1)} %select_reduce_fusion), kind=kLoop, calls=%fused_computation.36 | loop fusion | flops 127 | bytes 257 | tf_op jit(solution)/shard_map/jit(cholesky)/cholesky | solution.py:53
  49.4 0.7 %fusion.10 = f32[1,64,64]{2,1,0:T(8,128)S(1)} fusion(f32[64,64]{1,0:T(8,128)S(1)} %cholesky.17, pred[]{:T(512)} %compare_reduce_fusion), kind=kLoop, calls=%fused_computation.16 | loop fusion | flops 16384 | bytes 32769 | tf_op jit(solution)/shard_map/jit(_cho_solve)/triangular_solve | solution.py:54
  50.1 4.9 %custom-call.10 = f32[1,64,64]{1,2,0:T(8,128)S(1)} custom-call(f32[1,64,64]{2,1,0:T(8,128)S(1)} %fusion.10), custom_call_target="InvertDiagBlocksLowerTriangular" | custom-call | tf_op jit(solution)/shard_map/jit(_cho_solve)/triangular_solve | solution.py:54
  55.0 0.2 fusion.13
  55.1 0.2 fusion.11
  55.3 0.6 %dynamic-slice_multiply_fusion = f32[8,16]{1,0:T(8,128)} fusion(f32[64,16]{1,0:T(8,128)S(1)} %fusion.11, s32[]{:T(128)S(6)} %select_n.12), kind=kLoop, calls=%fused_computation.30 | loop fusion | flops 128 | bytes 1028 | tf_op jit(solution)/shard_map/mul | solution.py:57
  (9 shorter events, 0.1 us)
Async XLA Ops:
  0.0 3.0 %copy-start = (bf16[1,128,7168]{2,1,0:T(8,128)(2,1)S(1)}, bf16[1,128,7168]{2,1,0:T(8,128)(2,1)}, u32[]{:S(2)}) copy-start(bf16[1,128,7168]{2,1,0:T(8,128)(2,1)} %param.11) | copy-start | bytes 5505028
  0.0 3.0 %copy-start.1 = (bf16[7168,32]{0,1:T(8,128)(2,1)S(1)}, bf16[7168,32]{0,1:T(8,128)(2,1)}, u32[]{:S(2)}) copy-start(bf16[7168,32]{0,1:T(8,128)(2,1)} %param.19) | copy-start | bytes 1376260
  0.0 3.8 %copy-start.3 = (bf16[2048,32]{0,1:T(8,128)(2,1)S(1)}, bf16[2048,32]{0,1:T(8,128)(2,1)}, u32[]{:S(2)}) copy-start(bf16[2048,32]{0,1:T(8,128)(2,1)} %param.18) | copy-start | bytes 393220
  0.0 3.8 %copy-start.2 = (bf16[1,128,2048]{2,1,0:T(8,128)(2,1)S(1)}, bf16[1,128,2048]{2,1,0:T(8,128)(2,1)}, u32[]{:S(2)}) copy-start(bf16[1,128,2048]{2,1,0:T(8,128)(2,1)} %param.10) | copy-start | bytes 1572868
  1.8 6.2 %copy-start.6 = (s32[1,64]{1,0:T(1,128)S(1)}, s32[1,64]{1,0:T(1,128)}, u32[]{:S(2)}) copy-start(s32[1,64]{1,0:T(1,128)} %param.17) | copy-start | bytes 772
  3.0 5.1 %copy-start.4 = (s32[1,64]{1,0:T(1,128)S(1)}, s32[1,64]{1,0:T(1,128)}, u32[]{:S(2)}) copy-start(s32[1,64]{1,0:T(1,128)} %param.16) | copy-start | bytes 772
  3.1 5.4 %copy-start.7 = (s32[1,128]{1,0:T(1,128)S(1)}, s32[1,128]{1,0:T(1,128)}, u32[]{:S(2)}) copy-start(s32[1,128]{1,0:T(1,128)} %param.13) | copy-start | bytes 1540
  3.1 5.5 %copy-start.5 = (s32[1,128]{1,0:T(1,128)S(1)}, s32[1,128]{1,0:T(1,128)}, u32[]{:S(2)}) copy-start(s32[1,128]{1,0:T(1,128)} %param.12) | copy-start | bytes 1540

commit v2 on v1

v2 whole, which is shorter than its diff:
```python
import functools

import jax
import jax.numpy as jnp
from jax import lax
from jax.experimental import pallas as pl
from jax.experimental.pallas import tpu as pltpu
from jax.sharding import PartitionSpec as P

EX_DEV = 8
TEX_DEV = 4
ROWS = 16
F32 = jnp.float32
BF16 = jnp.bfloat16
NT = (((1,), (1,)), ((), ()))
NN = (((1,), (0,)), ((), ()))
VMEM = pl.BlockSpec(memory_space=pltpu.VMEM)
SMEM = pl.BlockSpec(memory_space=pltpu.SMEM)
HBM = pl.BlockSpec(memory_space=pltpu.HBM)


def split(x):
    hi = x.astype(BF16)
    rest = x - hi.astype(F32)
    mid = rest.astype(BF16)
    low = (rest - mid.astype(F32)).astype(BF16)
    return hi, mid, low


def mm(a, b, dims):
    return lax.dot_general(a, b, dims, preferred_element_type=F32)


def chunks_of(total, parts):
    size = total // parts
    return [(n * size, size) for n in range(parts)]


def project_kernel(ta, tg, sa, sg, pin, pout, out, acts, grads, win, wout, sems):
    rows = ta.shape[0]
    both = acts.shape[0]
    copies = []

    def copy(src, dst):
        dma = pltpu.make_async_copy(src, dst, sems.at[len(copies)])
        dma.start()
        copies.append(dma)
        return dma

    first = [
        copy(pin, win),
        copy(ta, acts.at[pl.ds(0, rows)]),
        copy(sa, acts.at[pl.ds(rows, both - rows)]),
        copy(pout, wout),
    ]
    later = []
    for start, size in chunks_of(grads.shape[1], 4):
        cols = pl.ds(start, size)
        later.append(
            (
                copy(tg.at[:, cols], grads.at[pl.ds(0, rows), cols]),
                copy(sg.at[:, cols], grads.at[pl.ds(rows, both - rows), cols]),
                start,
                size,
            )
        )
    for dma in first[:3]:
        dma.wait()
    xp = mm(acts[...], win[...], NT)
    first[3].wait()
    gp = None
    for one, two, start, size in later:
        one.wait()
        two.wait()
        cols = slice(start, start + size)
        part = mm(grads[:, cols], wout[:, cols], NT)
        gp = part if gp is None else gp + part
    rin = xp.shape[1]
    out[:, :rin] = xp
    out[:, rin:] = gp


def project(ta, tg, sa, sg, pin, pout):
    both = ta.shape[0] + sa.shape[0]
    rin, rout = pin.shape[0], pout.shape[0]
    return pl.pallas_call(
        project_kernel,
        out_shape=jax.ShapeDtypeStruct((both, rin + rout), F32),
        in_specs=[HBM] * 6,
        out_specs=VMEM,
        scratch_shapes=[
            pltpu.VMEM((both, ta.shape[1]), BF16),
            pltpu.VMEM((both, tg.shape[1]), BF16),
            pltpu.VMEM(pin.shape, BF16),
            pltpu.VMEM(pout.shape, BF16),
            pltpu.SemaphoreType.DMA((12,)),
        ],
        compiler_params=pltpu.CompilerParams(vmem_limit_bytes=60 << 20),
        name="project",
    )(ta, tg, sa, sg, pin, pout)


def gradient_kernel(own, other, tseg, tmask, sseg, smask, out):
    rin = 32
    full = own[...] + other[...]
    both, feats = full.shape
    width = out.shape[1]
    rout = width // rin
    row = lax.broadcasted_iota(jnp.int32, (feats, width), 0)
    col = lax.broadcasted_iota(jnp.int32, (feats, width), 1)
    spread_x = (row == col // rout).astype(BF16)
    spread_g = (row - rin == col[:, :] % rout).astype(BF16)
    parts = split(full)
    xrep = sum(mm(part, spread_x, NN) for part in parts[::-1])
    grep = sum(mm(part, spread_g[:, :128], NN) for part in parts[::-1])
    tokens = tseg.shape[1]
    test_row = EX_DEV + TEX_DEV * lax.rem(lax.axis_index("test"), 2)
    label = jnp.concatenate([tseg[...], sseg[...] + test_row], axis=1)
    keep = jnp.concatenate([tmask[...], smask[...]], axis=1)
    ex = lax.broadcasted_iota(jnp.int32, (ROWS, both), 0)
    weight = jnp.where(ex == label, keep, 0).astype(F32).astype(BF16)
    for start in range(0, width, 128):
        outer = xrep[:, start : start + 128] * grep
        out[:, start : start + 128] = sum(mm(weight, part, NN) for part in split(outer)[::-1])


def gradients(own, other, tseg, tmask, sseg, smask):
    return pl.pallas_call(
        gradient_kernel,
        out_shape=jax.ShapeDtypeStruct((ROWS, 1024), F32),
        in_specs=[VMEM] * 6,
        out_specs=VMEM,
        compiler_params=pltpu.CompilerParams(vmem_limit_bytes=16 << 20),
        name="gradients",
    )(own, other, tseg, tmask, sseg, smask)


def score_kernel(peers, near, own, *refs):
    mine = refs[:near]
    theirs = refs[near : 2 * near]
    out, train, test = refs[2 * near :]
    shard, core = lax.axis_index(("train", "test")), lax.axis_index("proj")
    shards = peers + 1

    def put(block, mask):
        slot = lax.rem(mask + shards - 1, shards)
        train[pl.ds(pl.multiple_of(slot * EX_DEV, EX_DEV), EX_DEV), :] = block[:EX_DEV, :]
        test[lax.bitwise_xor(shard, mask)] = block[EX_DEV:, :]

    for k in range(near):
        mask = jnp.where(core == 0, k + 1, (near + k + 1) % shards)
        put(mine[k], mask)
        put(theirs[k], jnp.where(core == 0, (near + k + 1) % shards, k + 1))
    put(own, 0)

    half = shards // 2
    pairs = [test[core * half + n] + test[core * half + n + 1] for n in range(0, half, 2)]
    rows = shards * EX_DEV
    tests = half * TEX_DEV
    x = jnp.concatenate([train[...]] + pairs, axis=0)
    hi, mid, _ = split(x)
    gram = mm(hi[:rows], hi, NT) + (mm(hi[:rows], mid, NT) + mm(mid[:rows], hi, NT))
    lane = lax.broadcasted_iota(jnp.int32, gram.shape, 1)
    line = lax.broadcasted_iota(jnp.int32, gram.shape, 0)
    gram = gram * (1.0 / rows) + jnp.where(lane == line, 1.0, 0.0)
    block = [gram[n * 8 : n * 8 + 8] for n in range(shards)]
    sub = lax.broadcasted_iota(jnp.int32, (8, 1), 0)
    for b in range(shards):
        for j in range(8):
            k = b * 8 + j
            pivot = block[b][j : j + 1, :]
            scaled = pivot / pivot[:, k : k + 1]
            for n in range(b, shards):
                col = block[n][:, k : k + 1]
                if n == b:
                    if b == shards - 1:
                        col = jnp.where(sub == j, 0.0, col)
                    else:
                        col = jnp.where(sub > j, col, 0.0)
                block[n] = block[n] - col * scaled
    last = block[-1]
    diag = jnp.sum(jnp.where(lane[:8] == sub + (rows - 8), last, 0.0), axis=1, keepdims=True)
    out[...] = last[:, rows:] / diag * (rows / 32.0)


def scores(own, mine, theirs, shards):
    near = len(mine)
    return pl.pallas_call(
        functools.partial(score_kernel, shards - 1, near),
        out_shape=jax.ShapeDtypeStruct((EX_DEV, shards * TEX_DEV // 2), F32),
        in_specs=[VMEM] * (1 + 2 * near),
        out_specs=VMEM,
        scratch_shapes=[
            pltpu.VMEM((shards * EX_DEV, 1024), F32),
            pltpu.VMEM((shards, ROWS - EX_DEV, 1024), F32),
        ],
        compiler_params=pltpu.CompilerParams(vmem_limit_bytes=16 << 20),
        name="scores",
    )(own, *mine, *theirs)


def large(own):
    shards = lax.axis_size(("train", "test"))
    total = EX_DEV * shards
    everyone = lax.all_gather(own, ("train", "test"), axis=0)
    width = own.shape[1]
    train_full = everyone[:, :EX_DEV].reshape(total, width)
    tests = everyone[:, EX_DEV : EX_DEV + TEX_DEV] + everyone[:, EX_DEV + TEX_DEV :]
    tests = tests.reshape(TEX_DEV * shards, width)
    cols = TEX_DEV * shards // lax.axis_size("proj")
    test_half = lax.dynamic_slice_in_dim(tests, lax.axis_index("proj") * cols, cols, 0)
    gram = jnp.dot(train_full, train_full.T, precision=lax.Precision.HIGHEST)
    cross = jnp.dot(train_full, test_half.T, precision=lax.Precision.HIGHEST)
    system = gram / total + jnp.eye(total, dtype=F32)
    factor = jnp.linalg.cholesky(system)
    solved = jax.scipy.linalg.cho_solve((factor, True), cross)
    row = lax.axis_index(("train", "test")) * EX_DEV
    return lax.dynamic_slice_in_dim(solved, row, EX_DEV, 0) / jnp.sqrt(F32(width))


def body(ta, tg, tseg, tmask, sa, sg, sseg, smask, pin, pout):
    shards = lax.axis_size(("train", "test"))
    part = project(ta[0], tg[0], sa[0], sg[0], pin.T, pout.T)
    other = lax.ppermute(part, "proj", [(0, 1), (1, 0)])
    own = gradients(part, other, tseg, tmask, sseg, smask)
    if shards != 8:
        return large(own)
    axes = ("train", "test", "proj")
    mine = []
    for first, second in ((1, 5), (2, 6), (3, 7), (4, 0)):
        route = [(i * 2, (i ^ first) * 2) for i in range(8)]
        if second:
            route += [(i * 2 + 1, (i ^ second) * 2 + 1) for i in range(8)]
        mine.append(lax.ppermute(own, axes, route))
    theirs = [lax.ppermute(x, "proj", [(0, 1), (1, 0)]) for x in mine]
    return scores(own, mine, theirs, shards)


def solution(mesh):
    return jax.shard_map(
        body,
        mesh=mesh,
        in_specs=(
            P(("groups", "train", "test"), None, "proj"),
            P(("groups", "train", "test"), None, "proj"),
            P(("groups", "train", "test"), None),
            P(("groups", "train", "test"), None),
            P(("groups", "train", "test"), None, "proj"),
            P(("groups", "train", "test"), None, "proj"),
            P(("groups", "train", "test"), None),
            P(("groups", "train", "test"), None),
            P("proj", None),
            P("proj", None),
        ),
        out_specs=P(("groups", "train", "test"), "proj"),
        check_vma=False,
    )
```

time: 56.1 us -> 28.7 us (0.51)
  blocking collectives: 36.9 us -> 0 us
  other arithmetic: 12.8 us -> 0 us
  Pallas kernels: 0 us -> 11.3 us
  starting transfers between devices: 0 us -> 10.2 us
  waiting for transfers between devices: 0 us -> 6.1 us
  matrix products: 5.7 us -> 0 us
  local copies, waits for them, and re-layouts: 0.22 us -> 0.9 us
    all_gather x1 -> x0, blocking collectives: 33 us -> none  [body(): lax.all_gather(jnp.concatenate([train_own, test_own], 0), ('train', 'test...]
    another operation x5 -> x0, other arithmetic: 12.1 us -> none  [the longest x3 6.52 us: body(): factor = jnp.linalg.cholesky(system)]
    pallas_call x0 -> x3, Pallas kernels: none -> 11.3 us  [the longest x1 6.36 us: scores(): pl.pallas_call(functools.partial(score_kernel, shards - 1, near), out_sha...]
    ppermute x0 -> x9, starting transfers between devices: none -> 10.2 us  [the longest x4 9.41 us: body(): mine.append(lax.ppermute(own, axes, route))]
    ppermute x0 -> x9, waiting for transfers between devices: none -> 6.1 us  [the longest x4 3.93 us: body(): mine.append(lax.ppermute(own, axes, route))]
    dot_general x8 -> x0, matrix products: 5.37 us -> none  [the longest x2 2.51 us: project(): jnp.dot(grads.reshape(rows, -1), proj_out, preferred_element_type=jnp.flo...]
    psum x1 -> x0, blocking collectives: 3.91 us -> none  [body(): lax.psum((train_xp, train_gp, test_xp, test_gp), 'proj')]
    unnamed x16 -> x10, local copies, waits for them, and re-layouts: 0.08 us -> 0.9 us
  transfers between devices with their start and end apart: 0 -> 9, of which waited for: 0 -> 7; matrix products, arithmetic and copies ran while one was open for 0% -> 0% of each run, Pallas kernels for 0% -> 0%
where the time goes in v2:
time: 28.7 us; the launch traced here: 28.6 us
  Pallas kernels  11.3 us (39%)
  starting transfers between devices  10.2 us (36%)
  waiting for transfers between devices  6.1 us (21%)
  local copies, waits for them, and re-layouts  0.9 us (3%)
    ppermute x4, starting transfers between devices, body(): mine.append(lax.ppermute(own, axes, route))  9.41 us
    pallas_call x1, Pallas kernels, scores(): pl.pallas_call(functools.partial(score_kernel, shards - 1, near), out_sha...  6.36 us
    pallas_call x1, Pallas kernels, project(): pl.pallas_call(project_kernel, out_shape=jax.ShapeDtypeStruct((both, rin...  4.07 us
    ppermute x4, waiting for transfers between devices, body(): mine.append(lax.ppermute(own, axes, route))  3.93 us
    ppermute x1, waiting for transfers between devices, body(): other = lax.ppermute(part, 'proj', [(0, 1), (1, 0)])  1.15 us
    ppermute x4, waiting for transfers between devices, body(): theirs = [lax.ppermute(x, 'proj', [(0, 1), (1, 0)]) for x in mine]  1.01 us
    unnamed x10, local copies, waits for them, and re-layouts  0.9 us
    pallas_call x1, Pallas kernels, gradients(): pl.pallas_call(gradient_kernel, out_shape=jax.ShapeDtypeStruct((ROWS, 102...  0.9 us
  transfers between devices with their start and end apart: 9, of which 7 were waited for; matrix products, arithmetic and copies ran while one was open for 0% of the time, Pallas kernels for 0%

profile of v2, /device:TPU:0, one launch (start us, length us, event | category | flops | bytes accessed | tf_op | source)
XLA Modules:
  0.0 28.6 jit_solution(11106369133675869324)
XLA Ops:
  0.0 0.0 copy-start.1
  0.0 0.0 copy-start.2
  0.0 0.0 copy-start.3
  0.0 0.0 copy-start.4
  0.0 4.1 %project.1.own = f32[192,64]{1,0:T(8,128)} custom-call(bf16[128,2048]{1,0:T(8,128)(2,1)} %bitcast.8, bf16[128,7168]{1,0:T(8,128)(2,1)} %bitcast.6, bf16[64,2048]{1,0:T(8,128)(2,1)} %bitcast.10, bf16[64,7168]{1,0:T(8,128)(2,1)} %bitcast.7, bf16[32,2048]{1,0:T(8,128)(2,1)} %bitcast.11, bf16[32,7168]{1,0:T(8,128)(2,1)} %bitcast.9), custom_call_target="tpu_custom_call" | custom-call | tf_op jit(solution)/shard_map/project/pallas_call | solution.py:86
  4.1 0.5 %collective-permute-start = (f32[192,64]{1,0:T(8,128)}, f32[192,64]{1,0:T(8,128)S(1)}, u32[]{:S(2)}, u32[]{:S(2)}) collective-permute-start(f32[192,64]{1,0:T(8,128)} %project.1.own), channel_id=1, source_target_pairs={{0,1},{1,0},{2,3},{3,2},{4,5},{5,4},{6,7},{7,6},{8,9},{9,8},{10,11... | collective-permute-start | bytes 147464 | tf_op jit(solution)/shard_map/ppermute | solution.py:224
  4.6 1.2 %collective-permute-done.other = f32[192,64]{1,0:T(8,128)S(1)} collective-permute-done((f32[192,64]{1,0:T(8,128)}, f32[192,64]{1,0:T(8,128)S(1)}, u32[]{:S(2)}, u32[]{:S(2)}) %collective-permute-start) | collective-permute-done | bytes 49184 | tf_op jit(solution)/shard_map/ppermute | solution.py:224
  5.8 0.0 copy-done.1
  5.8 0.0 copy-done.2
  5.8 0.0 copy-done.3
  5.8 0.0 copy-done.4
  5.8 0.0 copy-start
  5.8 0.9 %copy-done = f32[192,64]{1,0:T(8,128)S(1)} copy-done((f32[192,64]{1,0:T(8,128)S(1)}, f32[192,64]{1,0:T(8,128)}, u32[]{:S(2)}) %copy-start) | copy-done | bytes 49176
  6.7 0.9 %gradients.1.own = f32[16,1024]{1,0:T(8,128)S(1)} custom-call(f32[192,64]{1,0:T(8,128)S(1)} %copy-done, f32[192,64]{1,0:T(8,128)S(1)} %collective-permute-done.other, s32[1,128]{1,0:T(1,128)S(1)} %copy-done.1, s32[1,128]{1,0:T(1,128)S(1)} %copy-done.2, s32[1,64]{1,0:T(1,128)S(1)} %copy-done.3, s32[1,64]{1,0:T(1,128)S(1)} %copy-done.4), custom_call_target="tpu_custom_call" | custom-call | tf_op jit(solution)/shard_map/gradients/pallas_call | solution.py:128
  7.6 5.9 %collective-permute-start.4 = (f32[16,1024]{1,0:T(8,128)S(1)}, f32[16,1024]{1,0:T(8,128)S(1)}, u32[]{:S(2)}, u32[]{:S(2)}) collective-permute-start(f32[16,1024]{1,0:T(8,128)S(1)} %gradients.1.own), channel_id=1, source_target_pairs={{0,8},{2,10},{4,12},{6,14},{8,0},{10,2},{12,4},{14,6},{16,24},{18,... | collective-permute-start | bytes 196616 | tf_op jit(solution)/shard_map/ppermute | solution.py:234
  13.4 2.6 %collective-permute-start.3 = (f32[16,1024]{1,0:T(8,128)S(1)}, f32[16,1024]{1,0:T(8,128)S(1)}, u32[]{:S(2)}, u32[]{:S(2)}) collective-permute-start(f32[16,1024]{1,0:T(8,128)S(1)} %gradients.1.own), channel_id=1, source_target_pairs={{0,6},{2,4},{4,2},{6,0},{8,14},{10,12},{12,10},{14,8},{1,15},{3,13... | collective-permute-start | bytes 196616 | tf_op jit(solution)/shard_map/ppermute | solution.py:234
  16.0 0.4 %collective-permute-start.2 = (f32[16,1024]{1,0:T(8,128)S(1)}, f32[16,1024]{1,0:T(8,128)S(1)}, u32[]{:S(2)}, u32[]{:S(2)}) collective-permute-start(f32[16,1024]{1,0:T(8,128)S(1)} %gradients.1.own), channel_id=1, source_target_pairs={{0,4},{2,6},{4,0},{6,2},{8,12},{10,14},{12,8},{14,10},{1,13},{3,15... | collective-permute-start | bytes 196616 | tf_op jit(solution)/shard_map/ppermute | solution.py:234
  16.4 0.5 %collective-permute-start.1 = (f32[16,1024]{1,0:T(8,128)S(1)}, f32[16,1024]{1,0:T(8,128)S(1)}, u32[]{:S(2)}, u32[]{:S(2)}) collective-permute-start(f32[16,1024]{1,0:T(8,128)S(1)} %gradients.1.own), channel_id=1, source_target_pairs={{0,2},{2,0},{4,6},{6,4},{8,10},{10,8},{12,14},{14,12},{1,11},{3,9}... | collective-permute-start | bytes 196616 | tf_op jit(solution)/shard_map/ppermute | solution.py:234
  17.0 0.7 %collective-permute-done.4.refs_3_ = f32[16,1024]{1,0:T(8,128)S(1)} collective-permute-done((f32[16,1024]{1,0:T(8,128)S(1)}, f32[16,1024]{1,0:T(8,128)S(1)}, u32[]{:S(2)}, u32[]{:S(2)}) %collective-permute-start.4) | collective-permute-done | bytes 65568 | tf_op jit(solution)/shard_map/ppermute | solution.py:234
  17.7 0.0 collective-permute-start.8
  17.7 2.0 %collective-permute-done.3.refs_2_ = f32[16,1024]{1,0:T(8,128)S(1)} collective-permute-done((f32[16,1024]{1,0:T(8,128)S(1)}, f32[16,1024]{1,0:T(8,128)S(1)}, u32[]{:S(2)}, u32[]{:S(2)}) %collective-permute-start.3) | collective-permute-done | bytes 65568 | tf_op jit(solution)/shard_map/ppermute | solution.py:234
  19.7 0.0 collective-permute-start.7
  19.7 1.0 %collective-permute-done.2.refs_1_ = f32[16,1024]{1,0:T(8,128)S(1)} collective-permute-done((f32[16,1024]{1,0:T(8,128)S(1)}, f32[16,1024]{1,0:T(8,128)S(1)}, u32[]{:S(2)}, u32[]{:S(2)}) %collective-permute-start.2) | collective-permute-done | bytes 65568 | tf_op jit(solution)/shard_map/ppermute | solution.py:234
  20.7 0.0 collective-permute-start.6
  20.7 0.3 collective-permute-done.1.refs_0_
  20.9 0.2 collective-permute-start.5
  21.2 0.0 collective-permute-done.8.refs_7_
  21.2 0.0 collective-permute-done.7.refs_6_
  21.2 0.7 %collective-permute-done.6.refs_5_ = f32[16,1024]{1,0:T(8,128)S(1)} collective-permute-done((f32[16,1024]{1,0:T(8,128)S(1)}, f32[16,1024]{1,0:T(8,128)S(1)}, u32[]{:S(2)}, u32[]{:S(2)}) %collective-permute-start.6) | collective-permute-done | bytes 65568 | tf_op jit(solution)/shard_map/ppermute | solution.py:235
  21.9 0.3 collective-permute-done.5.refs_4_
  22.2 6.4 %scores.1 = f32[8,16]{1,0:T(8,128)} custom-call(f32[16,1024]{1,0:T(8,128)S(1)} %gradients.1.own, f32[16,1024]{1,0:T(8,128)S(1)} %collective-permute-done.1.refs_0_, f32[16,1024]{1,0:T(8,128)S(1)} %collective-permute-done.2.refs_1_, f32[16,1024]{1,0:T(8,128)S(1)} %collective-permute-done.3.refs_2_, f32[16,1024]{1,0:T(8,128)S(1)} %collective-permute-done.4.refs_3_, ...), custom_call_target="tpu_custom_call" | custom-call | tf_op jit(solution)/shard_map/scores/pallas_call | solution.py:188
Async XLA Ops:
  0.0 5.8 %copy-start.1 = (s32[1,128]{1,0:T(1,128)S(1)}, s32[1,128]{1,0:T(1,128)}, u32[]{:S(2)}) copy-start(s32[1,128]{1,0:T(1,128)} %tseg.1) | copy-start | bytes 1540
  0.0 5.8 %copy-start.2 = (s32[1,128]{1,0:T(1,128)S(1)}, s32[1,128]{1,0:T(1,128)}, u32[]{:S(2)}) copy-start(s32[1,128]{1,0:T(1,128)} %tmask.1) | copy-start | bytes 1540
  0.0 5.8 %copy-start.3 = (s32[1,64]{1,0:T(1,128)S(1)}, s32[1,64]{1,0:T(1,128)}, u32[]{:S(2)}) copy-start(s32[1,64]{1,0:T(1,128)} %sseg.1) | copy-start | bytes 772
  0.0 5.8 %copy-start.4 = (s32[1,64]{1,0:T(1,128)S(1)}, s32[1,64]{1,0:T(1,128)}, u32[]{:S(2)}) copy-start(s32[1,64]{1,0:T(1,128)} %smask.1) | copy-start | bytes 772
  4.1 1.7 %collective-permute-start = (f32[192,64]{1,0:T(8,128)}, f32[192,64]{1,0:T(8,128)S(1)}, u32[]{:S(2)}, u32[]{:S(2)}) collective-permute-start(f32[192,64]{1,0:T(8,128)} %project.1.own), channel_id=1, source_target_pairs={{0,1},{1,0},{2,3},{3,2},{4,5},{5,4},{6,7},{7,6},{8,9},{9,8},{10,11... | collective-permute-start | bytes 147464 | tf_op jit(solution)/shard_map/ppermute | solution.py:224
  5.8 0.9 %copy-start = (f32[192,64]{1,0:T(8,128)S(1)}, f32[192,64]{1,0:T(8,128)}, u32[]{:S(2)}) copy-start(f32[192,64]{1,0:T(8,128)} %project.1.own) | copy-start | bytes 147460
  7.6 10.1 %collective-permute-start.4 = (f32[16,1024]{1,0:T(8,128)S(1)}, f32[16,1024]{1,0:T(8,128)S(1)}, u32[]{:S(2)}, u32[]{:S(2)}) collective-permute-start(f32[16,1024]{1,0:T(8,128)S(1)} %gradients.1.own), channel_id=1, source_target_pairs={{0,8},{2,10},{4,12},{6,14},{8,0},{10,2},{12,4},{14,6},{16,24},{18,... | collective-permute-start | bytes 196616 | tf_op jit(solution)/shard_map/ppermute | solution.py:234
  13.4 6.2 %collective-permute-start.3 = (f32[16,1024]{1,0:T(8,128)S(1)}, f32[16,1024]{1,0:T(8,128)S(1)}, u32[]{:S(2)}, u32[]{:S(2)}) collective-permute-start(f32[16,1024]{1,0:T(8,128)S(1)} %gradients.1.own), channel_id=1, source_target_pairs={{0,6},{2,4},{4,2},{6,0},{8,14},{10,12},{12,10},{14,8},{1,15},{3,13... | collective-permute-start | bytes 196616 | tf_op jit(solution)/shard_map/ppermute | solution.py:234
  16.0 4.7 %collective-permute-start.2 = (f32[16,1024]{1,0:T(8,128)S(1)}, f32[16,1024]{1,0:T(8,128)S(1)}, u32[]{:S(2)}, u32[]{:S(2)}) collective-permute-start(f32[16,1024]{1,0:T(8,128)S(1)} %gradients.1.own), channel_id=1, source_target_pairs={{0,4},{2,6},{4,0},{6,2},{8,12},{10,14},{12,8},{14,10},{1,13},{3,15... | collective-permute-start | bytes 196616 | tf_op jit(solution)/shard_map/ppermute | solution.py:234
  16.4 4.5 %collective-permute-start.1 = (f32[16,1024]{1,0:T(8,128)S(1)}, f32[16,1024]{1,0:T(8,128)S(1)}, u32[]{:S(2)}, u32[]{:S(2)}) collective-permute-start(f32[16,1024]{1,0:T(8,128)S(1)} %gradients.1.own), channel_id=1, source_target_pairs={{0,2},{2,0},{4,6},{6,4},{8,10},{10,8},{12,14},{14,12},{1,11},{3,9}... | collective-permute-start | bytes 196616 | tf_op jit(solution)/shard_map/ppermute | solution.py:234
  17.7 3.5 %collective-permute-start.8 = (f32[16,1024]{1,0:T(8,128)S(1)}, f32[16,1024]{1,0:T(8,128)S(1)}, u32[]{:S(2)}, u32[]{:S(2)}) collective-permute-start(f32[16,1024]{1,0:T(8,128)S(1)} %collective-permute-done.4.refs_3_), channel_id=1, source_target_pairs={{0,1},{1,0},{2,3},{3,2},{4,5},{5,4},{6,7},{7,6},{8,9},{9,8},{10,11... | collective-permute-start | bytes 196616 | tf_op jit(solution)/shard_map/ppermute | solution.py:235
  19.7 1.5 %collective-permute-start.7 = (f32[16,1024]{1,0:T(8,128)S(1)}, f32[16,1024]{1,0:T(8,128)S(1)}, u32[]{:S(2)}, u32[]{:S(2)}) collective-permute-start(f32[16,1024]{1,0:T(8,128)S(1)} %collective-permute-done.3.refs_2_), channel_id=1, source_target_pairs={{0,1},{1,0},{2,3},{3,2},{4,5},{5,4},{6,7},{7,6},{8,9},{9,8},{10,11... | collective-permute-start | bytes 196616 | tf_op jit(solution)/shard_map/ppermute | solution.py:235
  20.7 1.3 %collective-permute-start.6 = (f32[16,1024]{1,0:T(8,128)S(1)}, f32[16,1024]{1,0:T(8,128)S(1)}, u32[]{:S(2)}, u32[]{:S(2)}) collective-permute-start(f32[16,1024]{1,0:T(8,128)S(1)} %collective-permute-done.2.refs_1_), channel_id=1, source_target_pairs={{0,1},{1,0},{2,3},{3,2},{4,5},{5,4},{6,7},{7,6},{8,9},{9,8},{10,11... | collective-permute-start | bytes 196616 | tf_op jit(solution)/shard_map/ppermute | solution.py:235
  20.9 1.3 %collective-permute-start.5 = (f32[16,1024]{1,0:T(8,128)S(1)}, f32[16,1024]{1,0:T(8,128)S(1)}, u32[]{:S(2)}, u32[]{:S(2)}) collective-permute-start(f32[16,1024]{1,0:T(8,128)S(1)} %collective-permute-done.1.refs_0_), channel_id=1, source_target_pairs={{0,1},{1,0},{2,3},{3,2},{4,5},{5,4},{6,7},{7,6},{8,9},{9,8},{10,11... | collective-permute-start | bytes 196616 | tf_op jit(solution)/shard_map/ppermute | solution.py:235

commit v3 on v2

--- a/solution.py
+++ b/solution.py
@@ -10,6 +10,7 @@
 EX_DEV = 8
 TEX_DEV = 4
 ROWS = 16
+ROUTES = ((4, 0), (3, 7), (2, 6), (1, 5))
 F32 = jnp.float32
 BF16 = jnp.bfloat16
 NT = (((1,), (1,)), ((), ()))
@@ -85,7 +86,7 @@
     rin, rout = pin.shape[0], pout.shape[0]
     return pl.pallas_call(
         project_kernel,
-        out_shape=jax.ShapeDtypeStruct((both, rin + rout), F32),
+        out_shape=pltpu.VMEM((both, rin + rout), F32),
         in_specs=[HBM] * 6,
         out_specs=VMEM,
         scratch_shapes=[
@@ -135,22 +136,21 @@
     )(own, other, tseg, tmask, sseg, smask)
 
 
-def score_kernel(peers, near, own, *refs):
+def score_kernel(routes, shards, own, *refs):
+    near = len(routes)
     mine = refs[:near]
     theirs = refs[near : 2 * near]
     out, train, test = refs[2 * near :]
     shard, core = lax.axis_index(("train", "test")), lax.axis_index("proj")
-    shards = peers + 1
 
     def put(block, mask):
         slot = lax.rem(mask + shards - 1, shards)
         train[pl.ds(pl.multiple_of(slot * EX_DEV, EX_DEV), EX_DEV), :] = block[:EX_DEV, :]
         test[lax.bitwise_xor(shard, mask)] = block[EX_DEV:, :]
 
-    for k in range(near):
-        mask = jnp.where(core == 0, k + 1, (near + k + 1) % shards)
-        put(mine[k], mask)
-        put(theirs[k], jnp.where(core == 0, (near + k + 1) % shards, k + 1))
+    for k, (first, second) in enumerate(routes):
+        put(mine[k], jnp.where(core == 0, first, second))
+        put(theirs[k], jnp.where(core == 0, second, first))
     put(own, 0)
 
     half = shards // 2
@@ -183,10 +183,10 @@
     out[...] = last[:, rows:] / diag * (rows / 32.0)
 
 
-def scores(own, mine, theirs, shards):
+def scores(own, mine, theirs, routes, shards):
     near = len(mine)
     return pl.pallas_call(
-        functools.partial(score_kernel, shards - 1, near),
+        functools.partial(score_kernel, routes, shards),
         out_shape=jax.ShapeDtypeStruct((EX_DEV, shards * TEX_DEV // 2), F32),
         in_specs=[VMEM] * (1 + 2 * near),
         out_specs=VMEM,
@@ -227,13 +227,11 @@
         return large(own)
     axes = ("train", "test", "proj")
     mine = []
-    for first, second in ((1, 5), (2, 6), (3, 7), (4, 0)):
-        route = [(i * 2, (i ^ first) * 2) for i in range(8)]
-        if second:
-            route += [(i * 2 + 1, (i ^ second) * 2 + 1) for i in range(8)]
+    for pair in ROUTES:
+        route = [(2 * i + c, 2 * (i ^ pair[c]) + c) for c in range(2) if pair[c] for i in range(shards)]
         mine.append(lax.ppermute(own, axes, route))
     theirs = [lax.ppermute(x, "proj", [(0, 1), (1, 0)]) for x in mine]
-    return scores(own, mine, theirs, shards)
+    return scores(own, mine, theirs, ROUTES, shards)
 
 
 def solution(mesh):

time: 28.7 us -> 25.9 us (0.902)
  waiting for transfers between devices: 6.1 us -> 2.55 us
  starting transfers between devices: 10.2 us -> 12.4 us
  local copies, waits for them, and re-layouts: 0.9 us -> 0.01 us
  Pallas kernels: 11.3 us -> 10.7 us
    ppermute x4, waiting for transfers between devices: 3.93 us -> 0.37 us  [body(): mine.append(lax.ppermute(own, axes, route))]
    ppermute x4, starting transfers between devices: 0.25 us -> 2.51 us  [body(): theirs = [lax.ppermute(x, 'proj', [(0, 1), (1, 0)]) for x in mine]]
    unnamed x10 -> x8, local copies, waits for them, and re-layouts: 0.9 us -> 0.01 us
    pallas_call x2, Pallas kernels: 10.4 us -> 9.81 us  [the longest x1 6.36 us: scores(): pl.pallas_call(functools.partial(score_kernel, routes, shards), out_shape...]
  transfers between devices with their start and end apart: 9 -> 9, of which waited for: 7 -> 4; matrix products, arithmetic and copies ran while one was open for 0% -> 0% of each run, Pallas kernels for 0% -> 0%
where the time goes in v3:
time: 25.9 us; the launch traced here: 25.7 us
  starting transfers between devices  12.4 us (48%)
  Pallas kernels  10.7 us (41%)
  waiting for transfers between devices  2.55 us (10%)
    ppermute x4, starting transfers between devices, body(): mine.append(lax.ppermute(own, axes, route))  9.34 us
    pallas_call x1, Pallas kernels, scores(): pl.pallas_call(functools.partial(score_kernel, routes, shards), out_shape...  6.36 us
    pallas_call x1, Pallas kernels, project(): pl.pallas_call(project_kernel, out_shape=pltpu.VMEM((both, rin + rout), F...  3.45 us
    ppermute x4, starting transfers between devices, body(): theirs = [lax.ppermute(x, 'proj', [(0, 1), (1, 0)]) for x in mine]  2.51 us
    ppermute x4, waiting for transfers between devices, body(): theirs = [lax.ppermute(x, 'proj', [(0, 1), (1, 0)]) for x in mine]  1.24 us
    ppermute x1, waiting for transfers between devices, body(): other = lax.ppermute(part, 'proj', [(0, 1), (1, 0)])  0.94 us
    pallas_call x1, Pallas kernels, gradients(): pl.pallas_call(gradient_kernel, out_shape=jax.ShapeDtypeStruct((ROWS, 102...  0.9 us
  transfers between devices with their start and end apart: 9, of which 4 were waited for; matrix products, arithmetic and copies ran while one was open for 0% of the time, Pallas kernels for 0%

profile of v3, /device:TPU:0, one launch (start us, length us, event | category | flops | bytes accessed | tf_op | source)
XLA Modules:
  0.0 25.7 jit_solution(13615118438071644327)
XLA Ops:
  0.0 0.0 copy-start
  0.0 0.0 copy-start.1
  0.0 0.0 copy-start.2
  0.0 0.0 copy-start.3
  0.0 3.5 %project.1.own = f32[192,64]{1,0:T(8,128)S(1)} custom-call(bf16[128,2048]{1,0:T(8,128)(2,1)} %bitcast.8, bf16[128,7168]{1,0:T(8,128)(2,1)} %bitcast.6, bf16[64,2048]{1,0:T(8,128)(2,1)} %bitcast.10, bf16[64,7168]{1,0:T(8,128)(2,1)} %bitcast.7, bf16[32,2048]{1,0:T(8,128)(2,1)} %bitcast.11, bf16[32,7168]{1,0:T(8,128)(2,1)} %bitcast.9), custom_call_target="tpu_custom_call" | custom-call | tf_op jit(solution)/shard_map/project/pallas_call | solution.py:87
  3.5 0.5 %collective-permute-start = (f32[192,64]{1,0:T(8,128)S(1)}, f32[192,64]{1,0:T(8,128)S(1)}, u32[]{:S(2)}, u32[]{:S(2)}) collective-permute-start(f32[192,64]{1,0:T(8,128)S(1)} %project.1.own), channel_id=1, source_target_pairs={{0,1},{1,0},{2,3},{3,2},{4,5},{5,4},{6,7},{7,6},{8,9},{9,8},{10,11... | collective-permute-start | bytes 147464 | tf_op jit(solution)/shard_map/ppermute | solution.py:224
  4.0 0.9 %collective-permute-done.other = f32[192,64]{1,0:T(8,128)S(1)} collective-permute-done((f32[192,64]{1,0:T(8,128)S(1)}, f32[192,64]{1,0:T(8,128)S(1)}, u32[]{:S(2)}, u32[]{:S(2)}) %collective-permute-start) | collective-permute-done | bytes 49184 | tf_op jit(solution)/shard_map/ppermute | solution.py:224
  4.9 0.0 copy-done
  4.9 0.0 copy-done.1
  4.9 0.0 copy-done.2
  4.9 0.0 copy-done.3
  4.9 0.9 %gradients.1.own = f32[16,1024]{1,0:T(8,128)S(1)} custom-call(f32[192,64]{1,0:T(8,128)S(1)} %project.1.own, f32[192,64]{1,0:T(8,128)S(1)} %collective-permute-done.other, s32[1,128]{1,0:T(1,128)S(1)} %copy-done, s32[1,128]{1,0:T(1,128)S(1)} %copy-done.1, s32[1,64]{1,0:T(1,128)S(1)} %copy-done.2, s32[1,64]{1,0:T(1,128)S(1)} %copy-done.3), custom_call_target="tpu_custom_call" | custom-call | tf_op jit(solution)/shard_map/gradients/pallas_call | solution.py:129
  5.8 2.9 %collective-permute-start.4 = (f32[16,1024]{1,0:T(8,128)S(1)}, f32[16,1024]{1,0:T(8,128)S(1)}, u32[]{:S(2)}, u32[]{:S(2)}) collective-permute-start(f32[16,1024]{1,0:T(8,128)S(1)} %gradients.1.own), channel_id=1, source_target_pairs={{0,2},{2,0},{4,6},{6,4},{8,10},{10,8},{12,14},{14,12},{1,11},{3,9}... | collective-permute-start | bytes 196616 | tf_op jit(solution)/shard_map/ppermute | solution.py:232
  8.7 1.6 %collective-permute-start.3 = (f32[16,1024]{1,0:T(8,128)S(1)}, f32[16,1024]{1,0:T(8,128)S(1)}, u32[]{:S(2)}, u32[]{:S(2)}) collective-permute-start(f32[16,1024]{1,0:T(8,128)S(1)} %gradients.1.own), channel_id=1, source_target_pairs={{0,4},{2,6},{4,0},{6,2},{8,12},{10,14},{12,8},{14,10},{1,13},{3,15... | collective-permute-start | bytes 196616 | tf_op jit(solution)/shard_map/ppermute | solution.py:232
  10.3 0.0 collective-permute-start.2
  10.3 4.9 %collective-permute-start.1 = (f32[16,1024]{1,0:T(8,128)S(1)}, f32[16,1024]{1,0:T(8,128)S(1)}, u32[]{:S(2)}, u32[]{:S(2)}) collective-permute-start(f32[16,1024]{1,0:T(8,128)S(1)} %gradients.1.own), channel_id=1, source_target_pairs={{0,8},{2,10},{4,12},{6,14},{8,0},{10,2},{12,4},{14,6},{16,24},{18,... | collective-permute-start | bytes 196616 | tf_op jit(solution)/shard_map/ppermute | solution.py:232
  15.2 0.0 collective-permute-done.4.refs_3_
  15.2 0.1 collective-permute-start.8
  15.3 0.0 collective-permute-done.3.refs_2_
  15.3 0.5 %collective-permute-start.7 = (f32[16,1024]{1,0:T(8,128)S(1)}, f32[16,1024]{1,0:T(8,128)S(1)}, u32[]{:S(2)}, u32[]{:S(2)}) collective-permute-start(f32[16,1024]{1,0:T(8,128)S(1)} %collective-permute-done.3.refs_2_), channel_id=1, source_target_pairs={{0,1},{1,0},{2,3},{3,2},{4,5},{5,4},{6,7},{7,6},{8,9},{9,8},{10,11... | collective-permute-start | bytes 196616 | tf_op jit(solution)/shard_map/ppermute | solution.py:233
  15.8 0.4 %collective-permute-done.2.refs_1_ = f32[16,1024]{1,0:T(8,128)S(1)} collective-permute-done((f32[16,1024]{1,0:T(8,128)S(1)}, f32[16,1024]{1,0:T(8,128)S(1)}, u32[]{:S(2)}, u32[]{:S(2)}) %collective-permute-start.2) | collective-permute-done | bytes 65568 | tf_op jit(solution)/shard_map/ppermute | solution.py:232
  16.1 1.9 %collective-permute-start.6 = (f32[16,1024]{1,0:T(8,128)S(1)}, f32[16,1024]{1,0:T(8,128)S(1)}, u32[]{:S(2)}, u32[]{:S(2)}) collective-permute-start(f32[16,1024]{1,0:T(8,128)S(1)} %collective-permute-done.2.refs_1_), channel_id=1, source_target_pairs={{0,1},{1,0},{2,3},{3,2},{4,5},{5,4},{6,7},{7,6},{8,9},{9,8},{10,11... | collective-permute-start | bytes 196616 | tf_op jit(solution)/shard_map/ppermute | solution.py:233
  18.1 0.0 collective-permute-done.1.refs_0_
  18.1 0.0 collective-permute-start.5
  18.1 0.0 collective-permute-done.8.refs_7_
  18.1 0.0 collective-permute-done.7.refs_6_
  18.1 0.9 %collective-permute-done.6.refs_5_ = f32[16,1024]{1,0:T(8,128)S(1)} collective-permute-done((f32[16,1024]{1,0:T(8,128)S(1)}, f32[16,1024]{1,0:T(8,128)S(1)}, u32[]{:S(2)}, u32[]{:S(2)}) %collective-permute-start.6) | collective-permute-done | bytes 65568 | tf_op jit(solution)/shard_map/ppermute | solution.py:233
  19.0 0.4 %collective-permute-done.5.refs_4_ = f32[16,1024]{1,0:T(8,128)S(1)} collective-permute-done((f32[16,1024]{1,0:T(8,128)S(1)}, f32[16,1024]{1,0:T(8,128)S(1)}, u32[]{:S(2)}, u32[]{:S(2)}) %collective-permute-start.5) | collective-permute-done | bytes 65568 | tf_op jit(solution)/shard_map/ppermute | solution.py:233
  19.4 6.4 %scores.1 = f32[8,16]{1,0:T(8,128)} custom-call(f32[16,1024]{1,0:T(8,128)S(1)} %gradients.1.own, f32[16,1024]{1,0:T(8,128)S(1)} %collective-permute-done.1.refs_0_, f32[16,1024]{1,0:T(8,128)S(1)} %collective-permute-done.2.refs_1_, f32[16,1024]{1,0:T(8,128)S(1)} %collective-permute-done.3.refs_2_, f32[16,1024]{1,0:T(8,128)S(1)} %collective-permute-done.4.refs_3_, ...), custom_call_target="tpu_custom_call" | custom-call | tf_op jit(solution)/shard_map/scores/pallas_call | solution.py:188
Async XLA Ops:
  0.0 4.9 %copy-start = (s32[1,128]{1,0:T(1,128)S(1)}, s32[1,128]{1,0:T(1,128)}, u32[]{:S(2)}) copy-start(s32[1,128]{1,0:T(1,128)} %tseg.1) | copy-start | bytes 1540
  0.0 4.9 %copy-start.1 = (s32[1,128]{1,0:T(1,128)S(1)}, s32[1,128]{1,0:T(1,128)}, u32[]{:S(2)}) copy-start(s32[1,128]{1,0:T(1,128)} %tmask.1) | copy-start | bytes 1540
  0.0 4.9 %copy-start.2 = (s32[1,64]{1,0:T(1,128)S(1)}, s32[1,64]{1,0:T(1,128)}, u32[]{:S(2)}) copy-start(s32[1,64]{1,0:T(1,128)} %sseg.1) | copy-start | bytes 772
  0.0 4.9 %copy-start.3 = (s32[1,64]{1,0:T(1,128)S(1)}, s32[1,64]{1,0:T(1,128)}, u32[]{:S(2)}) copy-start(s32[1,64]{1,0:T(1,128)} %smask.1) | copy-start | bytes 772
  3.5 1.5 %collective-permute-start = (f32[192,64]{1,0:T(8,128)S(1)}, f32[192,64]{1,0:T(8,128)S(1)}, u32[]{:S(2)}, u32[]{:S(2)}) collective-permute-start(f32[192,64]{1,0:T(8,128)S(1)} %project.1.own), channel_id=1, source_target_pairs={{0,1},{1,0},{2,3},{3,2},{4,5},{5,4},{6,7},{7,6},{8,9},{9,8},{10,11... | collective-permute-start | bytes 147464 | tf_op jit(solution)/shard_map/ppermute | solution.py:224
  5.8 9.4 %collective-permute-start.4 = (f32[16,1024]{1,0:T(8,128)S(1)}, f32[16,1024]{1,0:T(8,128)S(1)}, u32[]{:S(2)}, u32[]{:S(2)}) collective-permute-start(f32[16,1024]{1,0:T(8,128)S(1)} %gradients.1.own), channel_id=1, source_target_pairs={{0,2},{2,0},{4,6},{6,4},{8,10},{10,8},{12,14},{14,12},{1,11},{3,9}... | collective-permute-start | bytes 196616 | tf_op jit(solution)/shard_map/ppermute | solution.py:232
  8.7 6.6 %collective-permute-start.3 = (f32[16,1024]{1,0:T(8,128)S(1)}, f32[16,1024]{1,0:T(8,128)S(1)}, u32[]{:S(2)}, u32[]{:S(2)}) collective-permute-start(f32[16,1024]{1,0:T(8,128)S(1)} %gradients.1.own), channel_id=1, source_target_pairs={{0,4},{2,6},{4,0},{6,2},{8,12},{10,14},{12,8},{14,10},{1,13},{3,15... | collective-permute-start | bytes 196616 | tf_op jit(solution)/shard_map/ppermute | solution.py:232
  10.3 5.9 %collective-permute-start.2 = (f32[16,1024]{1,0:T(8,128)S(1)}, f32[16,1024]{1,0:T(8,128)S(1)}, u32[]{:S(2)}, u32[]{:S(2)}) collective-permute-start(f32[16,1024]{1,0:T(8,128)S(1)} %gradients.1.own), channel_id=1, source_target_pairs={{0,6},{2,4},{4,2},{6,0},{8,14},{10,12},{12,10},{14,8},{1,15},{3,13... | collective-permute-start | bytes 196616 | tf_op jit(solution)/shard_map/ppermute | solution.py:232
  10.3 7.8 %collective-permute-start.1 = (f32[16,1024]{1,0:T(8,128)S(1)}, f32[16,1024]{1,0:T(8,128)S(1)}, u32[]{:S(2)}, u32[]{:S(2)}) collective-permute-start(f32[16,1024]{1,0:T(8,128)S(1)} %gradients.1.own), channel_id=1, source_target_pairs={{0,8},{2,10},{4,12},{6,14},{8,0},{10,2},{12,4},{14,6},{16,24},{18,... | collective-permute-start | bytes 196616 | tf_op jit(solution)/shard_map/ppermute | solution.py:232
  15.2 2.9 %collective-permute-start.8 = (f32[16,1024]{1,0:T(8,128)S(1)}, f32[16,1024]{1,0:T(8,128)S(1)}, u32[]{:S(2)}, u32[]{:S(2)}) collective-permute-start(f32[16,1024]{1,0:T(8,128)S(1)} %collective-permute-done.4.refs_3_), channel_id=1, source_target_pairs={{0,1},{1,0},{2,3},{3,2},{4,5},{5,4},{6,7},{7,6},{8,9},{9,8},{10,11... | collective-permute-start | bytes 196616 | tf_op jit(solution)/shard_map/ppermute | solution.py:233
  15.3 2.8 %collective-permute-start.7 = (f32[16,1024]{1,0:T(8,128)S(1)}, f32[16,1024]{1,0:T(8,128)S(1)}, u32[]{:S(2)}, u32[]{:S(2)}) collective-permute-start(f32[16,1024]{1,0:T(8,128)S(1)} %collective-permute-done.3.refs_2_), channel_id=1, source_target_pairs={{0,1},{1,0},{2,3},{3,2},{4,5},{5,4},{6,7},{7,6},{8,9},{9,8},{10,11... | collective-permute-start | bytes 196616 | tf_op jit(solution)/shard_map/ppermute | solution.py:233
  16.1 2.9 %collective-permute-start.6 = (f32[16,1024]{1,0:T(8,128)S(1)}, f32[16,1024]{1,0:T(8,128)S(1)}, u32[]{:S(2)}, u32[]{:S(2)}) collective-permute-start(f32[16,1024]{1,0:T(8,128)S(1)} %collective-permute-done.2.refs_1_), channel_id=1, source_target_pairs={{0,1},{1,0},{2,3},{3,2},{4,5},{5,4},{6,7},{7,6},{8,9},{9,8},{10,11... | collective-permute-start | bytes 196616 | tf_op jit(solution)/shard_map/ppermute | solution.py:233
  18.1 1.3 %collective-permute-start.5 = (f32[16,1024]{1,0:T(8,128)S(1)}, f32[16,1024]{1,0:T(8,128)S(1)}, u32[]{:S(2)}, u32[]{:S(2)}) collective-permute-start(f32[16,1024]{1,0:T(8,128)S(1)} %collective-permute-done.1.refs_0_), channel_id=1, source_target_pairs={{0,1},{1,0},{2,3},{3,2},{4,5},{5,4},{6,7},{7,6},{8,9},{9,8},{10,11... | collective-permute-start | bytes 196616 | tf_op jit(solution)/shard_map/ppermute | solution.py:233

commit v4 on v3

--- a/solution.py
+++ b/solution.py
@@ -136,6 +136,29 @@
     )(own, other, tseg, tmask, sseg, smask)
 
 
+def pivot_rows(block, first):
+    shape = block.shape
+    rows = [jnp.broadcast_to(block[i : i + 1, :], shape) for i in range(8)]
+    a = [[jnp.broadcast_to(rows[i][:, first + j : first + j + 1], shape) for j in range(i + 1)] for i in range(8)]
+    low = [[None] * 8 for _ in range(8)]
+    inverse = []
+    for j in range(8):
+        inverse.append(1.0 / a[j][j])
+        for i in range(j + 1, 8):
+            low[i][j] = a[i][j] * inverse[j]
+        for i in range(j + 1, 8):
+            for m in range(j + 1, i + 1):
+                a[i][m] = a[i][m] - low[i][j] * a[m][j]
+            rows[i] = rows[i] - low[i][j] * rows[j]
+    solved = [None] * 8
+    for i in range(7, -1, -1):
+        value = rows[i] * inverse[i]
+        for j in range(i + 1, 8):
+            value = value - low[j][i] * solved[j]
+        solved[i] = value
+    return solved
+
+
 def score_kernel(routes, shards, own, *refs):
     near = len(routes)
     mine = refs[:near]
@@ -164,23 +187,18 @@
     line = lax.broadcasted_iota(jnp.int32, gram.shape, 0)
     gram = gram * (1.0 / rows) + jnp.where(lane == line, 1.0, 0.0)
     block = [gram[n * 8 : n * 8 + 8] for n in range(shards)]
-    sub = lax.broadcasted_iota(jnp.int32, (8, 1), 0)
     for b in range(shards):
-        for j in range(8):
-            k = b * 8 + j
-            pivot = block[b][j : j + 1, :]
-            scaled = pivot / pivot[:, k : k + 1]
-            for n in range(b, shards):
-                col = block[n][:, k : k + 1]
-                if n == b:
-                    if b == shards - 1:
-                        col = jnp.where(sub == j, 0.0, col)
-                    else:
-                        col = jnp.where(sub > j, col, 0.0)
-                block[n] = block[n] - col * scaled
-    last = block[-1]
-    diag = jnp.sum(jnp.where(lane[:8] == sub + (rows - 8), last, 0.0), axis=1, keepdims=True)
-    out[...] = last[:, rows:] / diag * (rows / 32.0)
+        weights = pivot_rows(block[b], b * 8)
+        for n in range(b + 1, shards):
+            left = block[n]
+            for j, row in enumerate(weights):
+                left = left - block[n][:, b * 8 + j : b * 8 + j + 1] * row
+            block[n] = left
+    sub = lax.broadcasted_iota(jnp.int32, block[0].shape, 0)
+    own_rows = weights[0]
+    for i in range(1, 8):
+        own_rows = jnp.where(sub == i, weights[i], own_rows)
+    out[...] = own_rows[:, rows:] * (rows / 32.0)
 
 
 def scores(own, mine, theirs, routes, shards):

time: 25.9 us -> 23 us (0.89)
  Pallas kernels: 10.7 us -> 7.86 us
    pallas_call x1, Pallas kernels: 6.36 us -> 3.51 us  [scores(): pl.pallas_call(functools.partial(score_kernel, routes, shards), out_shape...]
where the time goes in v4:
time: 23 us; the launch traced here: 22.9 us
  starting transfers between devices  12.4 us (54%)
  Pallas kernels  7.86 us (34%)
  waiting for transfers between devices  2.55 us (11%)
    ppermute x4, starting transfers between devices, body(): mine.append(lax.ppermute(own, axes, route))  9.34 us
    pallas_call x1, Pallas kernels, scores(): pl.pallas_call(functools.partial(score_kernel, routes, shards), out_shape...  3.51 us
    pallas_call x1, Pallas kernels, project(): pl.pallas_call(project_kernel, out_shape=pltpu.VMEM((both, rin + rout), F...  3.45 us
    ppermute x4, starting transfers between devices, body(): theirs = [lax.ppermute(x, 'proj', [(0, 1), (1, 0)]) for x in mine]  2.51 us
    ppermute x4, waiting for transfers between devices, body(): theirs = [lax.ppermute(x, 'proj', [(0, 1), (1, 0)]) for x in mine]  1.24 us
    ppermute x1, waiting for transfers between devices, body(): other = lax.ppermute(part, 'proj', [(0, 1), (1, 0)])  0.94 us
    pallas_call x1, Pallas kernels, gradients(): pl.pallas_call(gradient_kernel, out_shape=jax.ShapeDtypeStruct((ROWS, 102...  0.9 us
    ppermute x1, starting transfers between devices, body(): other = lax.ppermute(part, 'proj', [(0, 1), (1, 0)])  0.52 us
  transfers between devices with their start and end apart: 9, of which 4 were waited for; matrix products, arithmetic and copies ran while one was open for 0% of the time, Pallas kernels for 0%

profile of v4, /device:TPU:0, one launch (start us, length us, event | category | flops | bytes accessed | tf_op | source)
XLA Modules:
  0.0 22.9 jit_solution(11473450756694409199)
XLA Ops:
  0.0 0.0 copy-start
  0.0 0.0 copy-start.1
  0.0 0.0 copy-start.2
  0.0 0.0 copy-start.3
  0.0 3.5 %project.1.own = f32[192,64]{1,0:T(8,128)S(1)} custom-call(bf16[128,2048]{1,0:T(8,128)(2,1)} %bitcast.8, bf16[128,7168]{1,0:T(8,128)(2,1)} %bitcast.6, bf16[64,2048]{1,0:T(8,128)(2,1)} %bitcast.10, bf16[64,7168]{1,0:T(8,128)(2,1)} %bitcast.7, bf16[32,2048]{1,0:T(8,128)(2,1)} %bitcast.11, bf16[32,7168]{1,0:T(8,128)(2,1)} %bitcast.9), custom_call_target="tpu_custom_call" | custom-call | tf_op jit(solution)/shard_map/project/pallas_call | solution.py:87
  3.5 0.5 %collective-permute-start = (f32[192,64]{1,0:T(8,128)S(1)}, f32[192,64]{1,0:T(8,128)S(1)}, u32[]{:S(2)}, u32[]{:S(2)}) collective-permute-start(f32[192,64]{1,0:T(8,128)S(1)} %project.1.own), channel_id=1, source_target_pairs={{0,1},{1,0},{2,3},{3,2},{4,5},{5,4},{6,7},{7,6},{8,9},{9,8},{10,11... | collective-permute-start | bytes 147464 | tf_op jit(solution)/shard_map/ppermute | solution.py:242
  4.0 0.9 %collective-permute-done.other = f32[192,64]{1,0:T(8,128)S(1)} collective-permute-done((f32[192,64]{1,0:T(8,128)S(1)}, f32[192,64]{1,0:T(8,128)S(1)}, u32[]{:S(2)}, u32[]{:S(2)}) %collective-permute-start) | collective-permute-done | bytes 49184 | tf_op jit(solution)/shard_map/ppermute | solution.py:242
  4.9 0.0 copy-done
  4.9 0.0 copy-done.1
  4.9 0.0 copy-done.2
  4.9 0.0 copy-done.3
  4.9 0.9 %gradients.1.own = f32[16,1024]{1,0:T(8,128)S(1)} custom-call(f32[192,64]{1,0:T(8,128)S(1)} %project.1.own, f32[192,64]{1,0:T(8,128)S(1)} %collective-permute-done.other, s32[1,128]{1,0:T(1,128)S(1)} %copy-done, s32[1,128]{1,0:T(1,128)S(1)} %copy-done.1, s32[1,64]{1,0:T(1,128)S(1)} %copy-done.2, s32[1,64]{1,0:T(1,128)S(1)} %copy-done.3), custom_call_target="tpu_custom_call" | custom-call | tf_op jit(solution)/shard_map/gradients/pallas_call | solution.py:129
  5.8 2.9 %collective-permute-start.4 = (f32[16,1024]{1,0:T(8,128)S(1)}, f32[16,1024]{1,0:T(8,128)S(1)}, u32[]{:S(2)}, u32[]{:S(2)}) collective-permute-start(f32[16,1024]{1,0:T(8,128)S(1)} %gradients.1.own), channel_id=1, source_target_pairs={{0,2},{2,0},{4,6},{6,4},{8,10},{10,8},{12,14},{14,12},{1,11},{3,9}... | collective-permute-start | bytes 196616 | tf_op jit(solution)/shard_map/ppermute | solution.py:250
  8.7 1.6 %collective-permute-start.3 = (f32[16,1024]{1,0:T(8,128)S(1)}, f32[16,1024]{1,0:T(8,128)S(1)}, u32[]{:S(2)}, u32[]{:S(2)}) collective-permute-start(f32[16,1024]{1,0:T(8,128)S(1)} %gradients.1.own), channel_id=1, source_target_pairs={{0,4},{2,6},{4,0},{6,2},{8,12},{10,14},{12,8},{14,10},{1,13},{3,15... | collective-permute-start | bytes 196616 | tf_op jit(solution)/shard_map/ppermute | solution.py:250
  10.3 0.0 collective-permute-start.2
  10.3 4.9 %collective-permute-start.1 = (f32[16,1024]{1,0:T(8,128)S(1)}, f32[16,1024]{1,0:T(8,128)S(1)}, u32[]{:S(2)}, u32[]{:S(2)}) collective-permute-start(f32[16,1024]{1,0:T(8,128)S(1)} %gradients.1.own), channel_id=1, source_target_pairs={{0,8},{2,10},{4,12},{6,14},{8,0},{10,2},{12,4},{14,6},{16,24},{18,... | collective-permute-start | bytes 196616 | tf_op jit(solution)/shard_map/ppermute | solution.py:250
  15.2 0.0 collective-permute-done.4.refs_3_
  15.2 0.1 collective-permute-start.8
  15.3 0.0 collective-permute-done.3.refs_2_
  15.3 0.5 %collective-permute-start.7 = (f32[16,1024]{1,0:T(8,128)S(1)}, f32[16,1024]{1,0:T(8,128)S(1)}, u32[]{:S(2)}, u32[]{:S(2)}) collective-permute-start(f32[16,1024]{1,0:T(8,128)S(1)} %collective-permute-done.3.refs_2_), channel_id=1, source_target_pairs={{0,1},{1,0},{2,3},{3,2},{4,5},{5,4},{6,7},{7,6},{8,9},{9,8},{10,11... | collective-permute-start | bytes 196616 | tf_op jit(solution)/shard_map/ppermute | solution.py:251
  15.8 0.4 %collective-permute-done.2.refs_1_ = f32[16,1024]{1,0:T(8,128)S(1)} collective-permute-done((f32[16,1024]{1,0:T(8,128)S(1)}, f32[16,1024]{1,0:T(8,128)S(1)}, u32[]{:S(2)}, u32[]{:S(2)}) %collective-permute-start.2) | collective-permute-done | bytes 65568 | tf_op jit(solution)/shard_map/ppermute | solution.py:250
  16.1 1.9 %collective-permute-start.6 = (f32[16,1024]{1,0:T(8,128)S(1)}, f32[16,1024]{1,0:T(8,128)S(1)}, u32[]{:S(2)}, u32[]{:S(2)}) collective-permute-start(f32[16,1024]{1,0:T(8,128)S(1)} %collective-permute-done.2.refs_1_), channel_id=1, source_target_pairs={{0,1},{1,0},{2,3},{3,2},{4,5},{5,4},{6,7},{7,6},{8,9},{9,8},{10,11... | collective-permute-start | bytes 196616 | tf_op jit(solution)/shard_map/ppermute | solution.py:251
  18.1 0.0 collective-permute-done.1.refs_0_
  18.1 0.0 collective-permute-start.5
  18.1 0.0 collective-permute-done.8.refs_7_
  18.1 0.0 collective-permute-done.7.refs_6_
  18.1 0.9 %collective-permute-done.6.refs_5_ = f32[16,1024]{1,0:T(8,128)S(1)} collective-permute-done((f32[16,1024]{1,0:T(8,128)S(1)}, f32[16,1024]{1,0:T(8,128)S(1)}, u32[]{:S(2)}, u32[]{:S(2)}) %collective-permute-start.6) | collective-permute-done | bytes 65568 | tf_op jit(solution)/shard_map/ppermute | solution.py:251
  19.0 0.4 %collective-permute-done.5.refs_4_ = f32[16,1024]{1,0:T(8,128)S(1)} collective-permute-done((f32[16,1024]{1,0:T(8,128)S(1)}, f32[16,1024]{1,0:T(8,128)S(1)}, u32[]{:S(2)}, u32[]{:S(2)}) %collective-permute-start.5) | collective-permute-done | bytes 65568 | tf_op jit(solution)/shard_map/ppermute | solution.py:251
  19.4 3.5 %scores.1 = f32[8,16]{1,0:T(8,128)} custom-call(f32[16,1024]{1,0:T(8,128)S(1)} %gradients.1.own, f32[16,1024]{1,0:T(8,128)S(1)} %collective-permute-done.1.refs_0_, f32[16,1024]{1,0:T(8,128)S(1)} %collective-permute-done.2.refs_1_, f32[16,1024]{1,0:T(8,128)S(1)} %collective-permute-done.3.refs_2_, f32[16,1024]{1,0:T(8,128)S(1)} %collective-permute-done.4.refs_3_, ...), custom_call_target="tpu_custom_call" | custom-call | tf_op jit(solution)/shard_map/scores/pallas_call | solution.py:206
Async XLA Ops:
  0.0 4.9 %copy-start = (s32[1,128]{1,0:T(1,128)S(1)}, s32[1,128]{1,0:T(1,128)}, u32[]{:S(2)}) copy-start(s32[1,128]{1,0:T(1,128)} %tseg.1) | copy-start | bytes 1540
  0.0 4.9 %copy-start.1 = (s32[1,128]{1,0:T(1,128)S(1)}, s32[1,128]{1,0:T(1,128)}, u32[]{:S(2)}) copy-start(s32[1,128]{1,0:T(1,128)} %tmask.1) | copy-start | bytes 1540
  0.0 4.9 %copy-start.2 = (s32[1,64]{1,0:T(1,128)S(1)}, s32[1,64]{1,0:T(1,128)}, u32[]{:S(2)}) copy-start(s32[1,64]{1,0:T(1,128)} %sseg.1) | copy-start | bytes 772
  0.0 4.9 %copy-start.3 = (s32[1,64]{1,0:T(1,128)S(1)}, s32[1,64]{1,0:T(1,128)}, u32[]{:S(2)}) copy-start(s32[1,64]{1,0:T(1,128)} %smask.1) | copy-start | bytes 772
  3.5 1.5 %collective-permute-start = (f32[192,64]{1,0:T(8,128)S(1)}, f32[192,64]{1,0:T(8,128)S(1)}, u32[]{:S(2)}, u32[]{:S(2)}) collective-permute-start(f32[192,64]{1,0:T(8,128)S(1)} %project.1.own), channel_id=1, source_target_pairs={{0,1},{1,0},{2,3},{3,2},{4,5},{5,4},{6,7},{7,6},{8,9},{9,8},{10,11... | collective-permute-start | bytes 147464 | tf_op jit(solution)/shard_map/ppermute | solution.py:242
  5.8 9.4 %collective-permute-start.4 = (f32[16,1024]{1,0:T(8,128)S(1)}, f32[16,1024]{1,0:T(8,128)S(1)}, u32[]{:S(2)}, u32[]{:S(2)}) collective-permute-start(f32[16,1024]{1,0:T(8,128)S(1)} %gradients.1.own), channel_id=1, source_target_pairs={{0,2},{2,0},{4,6},{6,4},{8,10},{10,8},{12,14},{14,12},{1,11},{3,9}... | collective-permute-start | bytes 196616 | tf_op jit(solution)/shard_map/ppermute | solution.py:250
  8.7 6.6 %collective-permute-start.3 = (f32[16,1024]{1,0:T(8,128)S(1)}, f32[16,1024]{1,0:T(8,128)S(1)}, u32[]{:S(2)}, u32[]{:S(2)}) collective-permute-start(f32[16,1024]{1,0:T(8,128)S(1)} %gradients.1.own), channel_id=1, source_target_pairs={{0,4},{2,6},{4,0},{6,2},{8,12},{10,14},{12,8},{14,10},{1,13},{3,15... | collective-permute-start | bytes 196616 | tf_op jit(solution)/shard_map/ppermute | solution.py:250
  10.3 5.9 %collective-permute-start.2 = (f32[16,1024]{1,0:T(8,128)S(1)}, f32[16,1024]{1,0:T(8,128)S(1)}, u32[]{:S(2)}, u32[]{:S(2)}) collective-permute-start(f32[16,1024]{1,0:T(8,128)S(1)} %gradients.1.own), channel_id=1, source_target_pairs={{0,6},{2,4},{4,2},{6,0},{8,14},{10,12},{12,10},{14,8},{1,15},{3,13... | collective-permute-start | bytes 196616 | tf_op jit(solution)/shard_map/ppermute | solution.py:250
  10.3 7.8 %collective-permute-start.1 = (f32[16,1024]{1,0:T(8,128)S(1)}, f32[16,1024]{1,0:T(8,128)S(1)}, u32[]{:S(2)}, u32[]{:S(2)}) collective-permute-start(f32[16,1024]{1,0:T(8,128)S(1)} %gradients.1.own), channel_id=1, source_target_pairs={{0,8},{2,10},{4,12},{6,14},{8,0},{10,2},{12,4},{14,6},{16,24},{18,... | collective-permute-start | bytes 196616 | tf_op jit(solution)/shard_map/ppermute | solution.py:250
  15.2 2.9 %collective-permute-start.8 = (f32[16,1024]{1,0:T(8,128)S(1)}, f32[16,1024]{1,0:T(8,128)S(1)}, u32[]{:S(2)}, u32[]{:S(2)}) collective-permute-start(f32[16,1024]{1,0:T(8,128)S(1)} %collective-permute-done.4.refs_3_), channel_id=1, source_target_pairs={{0,1},{1,0},{2,3},{3,2},{4,5},{5,4},{6,7},{7,6},{8,9},{9,8},{10,11... | collective-permute-start | bytes 196616 | tf_op jit(solution)/shard_map/ppermute | solution.py:251
  15.3 2.8 %collective-permute-start.7 = (f32[16,1024]{1,0:T(8,128)S(1)}, f32[16,1024]{1,0:T(8,128)S(1)}, u32[]{:S(2)}, u32[]{:S(2)}) collective-permute-start(f32[16,1024]{1,0:T(8,128)S(1)} %collective-permute-done.3.refs_2_), channel_id=1, source_target_pairs={{0,1},{1,0},{2,3},{3,2},{4,5},{5,4},{6,7},{7,6},{8,9},{9,8},{10,11... | collective-permute-start | bytes 196616 | tf_op jit(solution)/shard_map/ppermute | solution.py:251
  16.1 2.9 %collective-permute-start.6 = (f32[16,1024]{1,0:T(8,128)S(1)}, f32[16,1024]{1,0:T(8,128)S(1)}, u32[]{:S(2)}, u32[]{:S(2)}) collective-permute-start(f32[16,1024]{1,0:T(8,128)S(1)} %collective-permute-done.2.refs_1_), channel_id=1, source_target_pairs={{0,1},{1,0},{2,3},{3,2},{4,5},{5,4},{6,7},{7,6},{8,9},{9,8},{10,11... | collective-permute-start | bytes 196616 | tf_op jit(solution)/shard_map/ppermute | solution.py:251
  18.1 1.3 %collective-permute-start.5 = (f32[16,1024]{1,0:T(8,128)S(1)}, f32[16,1024]{1,0:T(8,128)S(1)}, u32[]{:S(2)}, u32[]{:S(2)}) collective-permute-start(f32[16,1024]{1,0:T(8,128)S(1)} %collective-permute-done.1.refs_0_), channel_id=1, source_target_pairs={{0,1},{1,0},{2,3},{3,2},{4,5},{5,4},{6,7},{7,6},{8,9},{9,8},{10,11... | collective-permute-start | bytes 196616 | tf_op jit(solution)/shard_map/ppermute | solution.py:251

commit v5 on v4

--- a/solution.py
+++ b/solution.py
@@ -10,7 +10,7 @@
 EX_DEV = 8
 TEX_DEV = 4
 ROWS = 16
-ROUTES = ((4, 0), (3, 7), (2, 6), (1, 5))
+ROUTES = ((4, 0), (1, 5), (2, 6), (3, 7))
 F32 = jnp.float32
 BF16 = jnp.bfloat16
 NT = (((1,), (1,)), ((), ()))
@@ -141,21 +141,28 @@
     rows = [jnp.broadcast_to(block[i : i + 1, :], shape) for i in range(8)]
     a = [[jnp.broadcast_to(rows[i][:, first + j : first + j + 1], shape) for j in range(i + 1)] for i in range(8)]
     low = [[None] * 8 for _ in range(8)]
-    inverse = []
-    for j in range(8):
-        inverse.append(1.0 / a[j][j])
-        for i in range(j + 1, 8):
-            low[i][j] = a[i][j] * inverse[j]
-        for i in range(j + 1, 8):
-            for m in range(j + 1, i + 1):
-                a[i][m] = a[i][m] - low[i][j] * a[m][j]
-            rows[i] = rows[i] - low[i][j] * rows[j]
+    pivots = []
+    for j in range(0, 8, 2):
+        p, q, r = a[j][j], a[j + 1][j], a[j + 1][j + 1]
+        scale = 1.0 / (p * r - q * q)
+        p, q, r = r * scale, q * scale, p * scale
+        pivots.append((p, q, r))
+        for i in range(j + 2, 8):
+            low[i][j] = a[i][j] * p - a[i][j + 1] * q
+            low[i][j + 1] = a[i][j + 1] * r - a[i][j] * q
+        for i in range(j + 2, 8):
+            for m in range(j + 2, i + 1):
+                a[i][m] = a[i][m] - (low[i][j] * a[m][j] + low[i][j + 1] * a[m][j + 1])
+            rows[i] = rows[i] - (low[i][j] * rows[j] + low[i][j + 1] * rows[j + 1])
     solved = [None] * 8
-    for i in range(7, -1, -1):
-        value = rows[i] * inverse[i]
-        for j in range(i + 1, 8):
-            value = value - low[j][i] * solved[j]
-        solved[i] = value
+    for j in range(6, -1, -2):
+        p, q, r = pivots[j // 2]
+        upper = rows[j] * p - rows[j + 1] * q
+        lower = rows[j + 1] * r - rows[j] * q
+        for i in range(j + 2, 8):
+            upper = upper - low[i][j] * solved[i]
+            lower = lower - low[i][j + 1] * solved[i]
+        solved[j], solved[j + 1] = upper, lower
     return solved
 
 

time: 23 us -> 22.5 us (0.978)
  Pallas kernels: 7.86 us -> 7.28 us
    pallas_call x1, Pallas kernels: 3.51 us -> 2.93 us  [scores(): pl.pallas_call(functools.partial(score_kernel, routes, shards), out_shape...]
where the time goes in v5:
time: 22.5 us; the launch traced here: 22.3 us
  starting transfers between devices  12.6 us (56%)
  Pallas kernels  7.28 us (32%)
  waiting for transfers between devices  2.38 us (11%)
    ppermute x4, starting transfers between devices, body(): mine.append(lax.ppermute(own, axes, route))  9.35 us
    pallas_call x1, Pallas kernels, project(): pl.pallas_call(project_kernel, out_shape=pltpu.VMEM((both, rin + rout), F...  3.45 us
    pallas_call x1, Pallas kernels, scores(): pl.pallas_call(functools.partial(score_kernel, routes, shards), out_shape...  2.93 us
    ppermute x4, starting transfers between devices, body(): theirs = [lax.ppermute(x, 'proj', [(0, 1), (1, 0)]) for x in mine]  2.72 us
    ppermute x4, waiting for transfers between devices, body(): theirs = [lax.ppermute(x, 'proj', [(0, 1), (1, 0)]) for x in mine]  1.25 us
    ppermute x1, waiting for transfers between devices, body(): other = lax.ppermute(part, 'proj', [(0, 1), (1, 0)])  0.94 us
    pallas_call x1, Pallas kernels, gradients(): pl.pallas_call(gradient_kernel, out_shape=jax.ShapeDtypeStruct((ROWS, 102...  0.9 us
    ppermute x1, starting transfers between devices, body(): other = lax.ppermute(part, 'proj', [(0, 1), (1, 0)])  0.52 us
  transfers between devices with their start and end apart: 9, of which 4 were waited for; matrix products, arithmetic and copies ran while one was open for 0% of the time, Pallas kernels for 0%

profile of v5, /device:TPU:0, one launch (start us, length us, event | category | flops | bytes accessed | tf_op | source)
XLA Modules:
  0.0 22.3 jit_solution(1429968587450667049)
XLA Ops:
  0.0 0.0 copy-start
  0.0 0.0 copy-start.1
  0.0 0.0 copy-start.2
  0.0 0.0 copy-start.3
  0.0 3.5 %project.1.own = f32[192,64]{1,0:T(8,128)S(1)} custom-call(bf16[128,2048]{1,0:T(8,128)(2,1)} %bitcast.8, bf16[128,7168]{1,0:T(8,128)(2,1)} %bitcast.6, bf16[64,2048]{1,0:T(8,128)(2,1)} %bitcast.10, bf16[64,7168]{1,0:T(8,128)(2,1)} %bitcast.7, bf16[32,2048]{1,0:T(8,128)(2,1)} %bitcast.11, bf16[32,7168]{1,0:T(8,128)(2,1)} %bitcast.9), custom_call_target="tpu_custom_call" | custom-call | tf_op jit(solution)/shard_map/project/pallas_call | solution.py:87
  3.5 0.5 %collective-permute-start = (f32[192,64]{1,0:T(8,128)S(1)}, f32[192,64]{1,0:T(8,128)S(1)}, u32[]{:S(2)}, u32[]{:S(2)}) collective-permute-start(f32[192,64]{1,0:T(8,128)S(1)} %project.1.own), channel_id=1, source_target_pairs={{0,1},{1,0},{2,3},{3,2},{4,5},{5,4},{6,7},{7,6},{8,9},{9,8},{10,11... | collective-permute-start | bytes 147464 | tf_op jit(solution)/shard_map/ppermute | solution.py:249
  4.0 0.9 %collective-permute-done.other = f32[192,64]{1,0:T(8,128)S(1)} collective-permute-done((f32[192,64]{1,0:T(8,128)S(1)}, f32[192,64]{1,0:T(8,128)S(1)}, u32[]{:S(2)}, u32[]{:S(2)}) %collective-permute-start) | collective-permute-done | bytes 49184 | tf_op jit(solution)/shard_map/ppermute | solution.py:249
  4.9 0.0 copy-done
  4.9 0.0 copy-done.1
  4.9 0.0 copy-done.2
  4.9 0.0 copy-done.3
  4.9 0.9 %gradients.1.own = f32[16,1024]{1,0:T(8,128)S(1)} custom-call(f32[192,64]{1,0:T(8,128)S(1)} %project.1.own, f32[192,64]{1,0:T(8,128)S(1)} %collective-permute-done.other, s32[1,128]{1,0:T(1,128)S(1)} %copy-done, s32[1,128]{1,0:T(1,128)S(1)} %copy-done.1, s32[1,64]{1,0:T(1,128)S(1)} %copy-done.2, s32[1,64]{1,0:T(1,128)S(1)} %copy-done.3), custom_call_target="tpu_custom_call" | custom-call | tf_op jit(solution)/shard_map/gradients/pallas_call | solution.py:129
  5.8 3.9 %collective-permute-start.4 = (f32[16,1024]{1,0:T(8,128)S(1)}, f32[16,1024]{1,0:T(8,128)S(1)}, u32[]{:S(2)}, u32[]{:S(2)}) collective-permute-start(f32[16,1024]{1,0:T(8,128)S(1)} %gradients.1.own), channel_id=1, source_target_pairs={{0,6},{2,4},{4,2},{6,0},{8,14},{10,12},{12,10},{14,8},{1,15},{3,13... | collective-permute-start | bytes 196616 | tf_op jit(solution)/shard_map/ppermute | solution.py:257
  9.7 0.4 %collective-permute-start.3 = (f32[16,1024]{1,0:T(8,128)S(1)}, f32[16,1024]{1,0:T(8,128)S(1)}, u32[]{:S(2)}, u32[]{:S(2)}) collective-permute-start(f32[16,1024]{1,0:T(8,128)S(1)} %gradients.1.own), channel_id=1, source_target_pairs={{0,4},{2,6},{4,0},{6,2},{8,12},{10,14},{12,8},{14,10},{1,13},{3,15... | collective-permute-start | bytes 196616 | tf_op jit(solution)/shard_map/ppermute | solution.py:257
  10.2 0.2 collective-permute-start.2
  10.3 4.9 %collective-permute-start.1 = (f32[16,1024]{1,0:T(8,128)S(1)}, f32[16,1024]{1,0:T(8,128)S(1)}, u32[]{:S(2)}, u32[]{:S(2)}) collective-permute-start(f32[16,1024]{1,0:T(8,128)S(1)} %gradients.1.own), channel_id=1, source_target_pairs={{0,8},{2,10},{4,12},{6,14},{8,0},{10,2},{12,4},{14,6},{16,24},{18,... | collective-permute-start | bytes 196616 | tf_op jit(solution)/shard_map/ppermute | solution.py:257
  15.2 0.0 collective-permute-done.4.refs_3_
  15.2 0.1 collective-permute-start.8
  15.3 0.0 collective-permute-done.3.refs_2_
  15.3 1.2 %collective-permute-start.7 = (f32[16,1024]{1,0:T(8,128)S(1)}, f32[16,1024]{1,0:T(8,128)S(1)}, u32[]{:S(2)}, u32[]{:S(2)}) collective-permute-start(f32[16,1024]{1,0:T(8,128)S(1)} %collective-permute-done.3.refs_2_), channel_id=1, source_target_pairs={{0,1},{1,0},{2,3},{3,2},{4,5},{5,4},{6,7},{7,6},{8,9},{9,8},{10,11... | collective-permute-start | bytes 196616 | tf_op jit(solution)/shard_map/ppermute | solution.py:258
  16.5 0.0 collective-permute-done.2.refs_1_
  16.5 1.4 %collective-permute-start.6 = (f32[16,1024]{1,0:T(8,128)S(1)}, f32[16,1024]{1,0:T(8,128)S(1)}, u32[]{:S(2)}, u32[]{:S(2)}) collective-permute-start(f32[16,1024]{1,0:T(8,128)S(1)} %collective-permute-done.2.refs_1_), channel_id=1, source_target_pairs={{0,1},{1,0},{2,3},{3,2},{4,5},{5,4},{6,7},{7,6},{8,9},{9,8},{10,11... | collective-permute-start | bytes 196616 | tf_op jit(solution)/shard_map/ppermute | solution.py:258
  17.9 0.2 collective-permute-done.1.refs_0_
  18.1 0.0 collective-permute-start.5
  18.1 0.0 collective-permute-done.8.refs_7_
  18.1 0.0 collective-permute-done.7.refs_6_
  18.1 0.7 %collective-permute-done.6.refs_5_ = f32[16,1024]{1,0:T(8,128)S(1)} collective-permute-done((f32[16,1024]{1,0:T(8,128)S(1)}, f32[16,1024]{1,0:T(8,128)S(1)}, u32[]{:S(2)}, u32[]{:S(2)}) %collective-permute-start.6) | collective-permute-done | bytes 65568 | tf_op jit(solution)/shard_map/ppermute | solution.py:258
  18.9 0.5 %collective-permute-done.5.refs_4_ = f32[16,1024]{1,0:T(8,128)S(1)} collective-permute-done((f32[16,1024]{1,0:T(8,128)S(1)}, f32[16,1024]{1,0:T(8,128)S(1)}, u32[]{:S(2)}, u32[]{:S(2)}) %collective-permute-start.5) | collective-permute-done | bytes 65568 | tf_op jit(solution)/shard_map/ppermute | solution.py:258
  19.4 2.9 %scores.1 = f32[8,16]{1,0:T(8,128)} custom-call(f32[16,1024]{1,0:T(8,128)S(1)} %gradients.1.own, f32[16,1024]{1,0:T(8,128)S(1)} %collective-permute-done.1.refs_0_, f32[16,1024]{1,0:T(8,128)S(1)} %collective-permute-done.2.refs_1_, f32[16,1024]{1,0:T(8,128)S(1)} %collective-permute-done.3.refs_2_, f32[16,1024]{1,0:T(8,128)S(1)} %collective-permute-done.4.refs_3_, ...), custom_call_target="tpu_custom_call" | custom-call | tf_op jit(solution)/shard_map/scores/pallas_call | solution.py:213
Async XLA Ops:
  0.0 4.9 %copy-start = (s32[1,128]{1,0:T(1,128)S(1)}, s32[1,128]{1,0:T(1,128)}, u32[]{:S(2)}) copy-start(s32[1,128]{1,0:T(1,128)} %tseg.1) | copy-start | bytes 1540
  0.0 4.9 %copy-start.1 = (s32[1,128]{1,0:T(1,128)S(1)}, s32[1,128]{1,0:T(1,128)}, u32[]{:S(2)}) copy-start(s32[1,128]{1,0:T(1,128)} %tmask.1) | copy-start | bytes 1540
  0.0 4.9 %copy-start.2 = (s32[1,64]{1,0:T(1,128)S(1)}, s32[1,64]{1,0:T(1,128)}, u32[]{:S(2)}) copy-start(s32[1,64]{1,0:T(1,128)} %sseg.1) | copy-start | bytes 772
  0.0 4.9 %copy-start.3 = (s32[1,64]{1,0:T(1,128)S(1)}, s32[1,64]{1,0:T(1,128)}, u32[]{:S(2)}) copy-start(s32[1,64]{1,0:T(1,128)} %smask.1) | copy-start | bytes 772
  3.5 1.5 %collective-permute-start = (f32[192,64]{1,0:T(8,128)S(1)}, f32[192,64]{1,0:T(8,128)S(1)}, u32[]{:S(2)}, u32[]{:S(2)}) collective-permute-start(f32[192,64]{1,0:T(8,128)S(1)} %project.1.own), channel_id=1, source_target_pairs={{0,1},{1,0},{2,3},{3,2},{4,5},{5,4},{6,7},{7,6},{8,9},{9,8},{10,11... | collective-permute-start | bytes 147464 | tf_op jit(solution)/shard_map/ppermute | solution.py:249
  5.8 9.4 %collective-permute-start.4 = (f32[16,1024]{1,0:T(8,128)S(1)}, f32[16,1024]{1,0:T(8,128)S(1)}, u32[]{:S(2)}, u32[]{:S(2)}) collective-permute-start(f32[16,1024]{1,0:T(8,128)S(1)} %gradients.1.own), channel_id=1, source_target_pairs={{0,6},{2,4},{4,2},{6,0},{8,14},{10,12},{12,10},{14,8},{1,15},{3,13... | collective-permute-start | bytes 196616 | tf_op jit(solution)/shard_map/ppermute | solution.py:257
  9.7 5.6 %collective-permute-start.3 = (f32[16,1024]{1,0:T(8,128)S(1)}, f32[16,1024]{1,0:T(8,128)S(1)}, u32[]{:S(2)}, u32[]{:S(2)}) collective-permute-start(f32[16,1024]{1,0:T(8,128)S(1)} %gradients.1.own), channel_id=1, source_target_pairs={{0,4},{2,6},{4,0},{6,2},{8,12},{10,14},{12,8},{14,10},{1,13},{3,15... | collective-permute-start | bytes 196616 | tf_op jit(solution)/shard_map/ppermute | solution.py:257
  10.2 6.4 %collective-permute-start.2 = (f32[16,1024]{1,0:T(8,128)S(1)}, f32[16,1024]{1,0:T(8,128)S(1)}, u32[]{:S(2)}, u32[]{:S(2)}) collective-permute-start(f32[16,1024]{1,0:T(8,128)S(1)} %gradients.1.own), channel_id=1, source_target_pairs={{0,2},{2,0},{4,6},{6,4},{8,10},{10,8},{12,14},{14,12},{1,11},{3,9}... | collective-permute-start | bytes 196616 | tf_op jit(solution)/shard_map/ppermute | solution.py:257
  10.3 7.8 %collective-permute-start.1 = (f32[16,1024]{1,0:T(8,128)S(1)}, f32[16,1024]{1,0:T(8,128)S(1)}, u32[]{:S(2)}, u32[]{:S(2)}) collective-permute-start(f32[16,1024]{1,0:T(8,128)S(1)} %gradients.1.own), channel_id=1, source_target_pairs={{0,8},{2,10},{4,12},{6,14},{8,0},{10,2},{12,4},{14,6},{16,24},{18,... | collective-permute-start | bytes 196616 | tf_op jit(solution)/shard_map/ppermute | solution.py:257
  15.2 2.9 %collective-permute-start.8 = (f32[16,1024]{1,0:T(8,128)S(1)}, f32[16,1024]{1,0:T(8,128)S(1)}, u32[]{:S(2)}, u32[]{:S(2)}) collective-permute-start(f32[16,1024]{1,0:T(8,128)S(1)} %collective-permute-done.4.refs_3_), channel_id=1, source_target_pairs={{0,1},{1,0},{2,3},{3,2},{4,5},{5,4},{6,7},{7,6},{8,9},{9,8},{10,11... | collective-permute-start | bytes 196616 | tf_op jit(solution)/shard_map/ppermute | solution.py:258
  15.3 2.8 %collective-permute-start.7 = (f32[16,1024]{1,0:T(8,128)S(1)}, f32[16,1024]{1,0:T(8,128)S(1)}, u32[]{:S(2)}, u32[]{:S(2)}) collective-permute-start(f32[16,1024]{1,0:T(8,128)S(1)} %collective-permute-done.3.refs_2_), channel_id=1, source_target_pairs={{0,1},{1,0},{2,3},{3,2},{4,5},{5,4},{6,7},{7,6},{8,9},{9,8},{10,11... | collective-permute-start | bytes 196616 | tf_op jit(solution)/shard_map/ppermute | solution.py:258
  16.5 2.3 %collective-permute-start.6 = (f32[16,1024]{1,0:T(8,128)S(1)}, f32[16,1024]{1,0:T(8,128)S(1)}, u32[]{:S(2)}, u32[]{:S(2)}) collective-permute-start(f32[16,1024]{1,0:T(8,128)S(1)} %collective-permute-done.2.refs_1_), channel_id=1, source_target_pairs={{0,1},{1,0},{2,3},{3,2},{4,5},{5,4},{6,7},{7,6},{8,9},{9,8},{10,11... | collective-permute-start | bytes 196616 | tf_op jit(solution)/shard_map/ppermute | solution.py:258
  18.1 1.3 %collective-permute-start.5 = (f32[16,1024]{1,0:T(8,128)S(1)}, f32[16,1024]{1,0:T(8,128)S(1)}, u32[]{:S(2)}, u32[]{:S(2)}) collective-permute-start(f32[16,1024]{1,0:T(8,128)S(1)} %collective-permute-done.1.refs_0_), channel_id=1, source_target_pairs={{0,1},{1,0},{2,3},{3,2},{4,5},{5,4},{6,7},{7,6},{8,9},{9,8},{10,11... | collective-permute-start | bytes 196616 | tf_op jit(solution)/shard_map/ppermute | solution.py:258

commit v6 on v5

--- a/solution.py
+++ b/solution.py
@@ -105,8 +105,8 @@
     rin = 32
     full = own[...] + other[...]
     both, feats = full.shape
-    width = out.shape[1]
-    rout = width // rin
+    rout = feats - rin
+    width = rin * rout
     row = lax.broadcasted_iota(jnp.int32, (feats, width), 0)
     col = lax.broadcasted_iota(jnp.int32, (feats, width), 1)
     spread_x = (row == col // rout).astype(BF16)
@@ -115,20 +115,29 @@
     xrep = sum(mm(part, spread_x, NN) for part in parts[::-1])
     grep = sum(mm(part, spread_g[:, :128], NN) for part in parts[::-1])
     tokens = tseg.shape[1]
-    test_row = EX_DEV + TEX_DEV * lax.rem(lax.axis_index("test"), 2)
-    label = jnp.concatenate([tseg[...], sseg[...] + test_row], axis=1)
     keep = jnp.concatenate([tmask[...], smask[...]], axis=1)
     ex = lax.broadcasted_iota(jnp.int32, (ROWS, both), 0)
-    weight = jnp.where(ex == label, keep, 0).astype(F32).astype(BF16)
+    weights = []
+    for side in range(2):
+        label = jnp.concatenate([tseg[...], sseg[...] + (EX_DEV + TEX_DEV * side)], axis=1)
+        weights.append(jnp.where(ex == label, keep, 0).astype(F32).astype(BF16))
+    half = width // 2
+    upper = {}
     for start in range(0, width, 128):
         outer = xrep[:, start : start + 128] * grep
-        out[:, start : start + 128] = sum(mm(weight, part, NN) for part in split(outer)[::-1])
+        side, place = divmod(start, half)
+        total = sum(mm(weights[side], part, NN) for part in split(outer)[::-1])
+        out[:, start : start + 128] = total[:EX_DEV]
+        if side == 0:
+            upper[place] = total[EX_DEV:]
+        else:
+            out[:, width + place : width + place + 128] = upper[place] + total[EX_DEV:]
 
 
 def gradients(own, other, tseg, tmask, sseg, smask):
     return pl.pallas_call(
         gradient_kernel,
-        out_shape=jax.ShapeDtypeStruct((ROWS, 1024), F32),
+        out_shape=jax.ShapeDtypeStruct((EX_DEV, 1536), F32),
         in_specs=[VMEM] * 6,
         out_specs=VMEM,
         compiler_params=pltpu.CompilerParams(vmem_limit_bytes=16 << 20),
@@ -175,8 +184,8 @@
 
     def put(block, mask):
         slot = lax.rem(mask + shards - 1, shards)
-        train[pl.ds(pl.multiple_of(slot * EX_DEV, EX_DEV), EX_DEV), :] = block[:EX_DEV, :]
-        test[lax.bitwise_xor(shard, mask)] = block[EX_DEV:, :]
+        train[pl.ds(pl.multiple_of(slot * EX_DEV, EX_DEV), EX_DEV), :] = block[:, :1024]
+        test[lax.bitwise_xor(shard, mask)] = block[:, 1024:]
 
     for k, (first, second) in enumerate(routes):
         put(mine[k], jnp.where(core == 0, first, second))
@@ -184,7 +193,13 @@
     put(own, 0)
 
     half = shards // 2
-    pairs = [test[core * half + n] + test[core * half + n + 1] for n in range(0, half, 2)]
+    first = lax.broadcasted_iota(jnp.int32, (EX_DEV, 512), 0) < TEX_DEV
+    pairs = []
+    for n in range(0, half, 2):
+        one, two = test[core * half + n], test[core * half + n + 1]
+        left = jnp.where(first, one, pltpu.roll(two, TEX_DEV, 0))
+        right = jnp.where(first, pltpu.roll(one, TEX_DEV, 0), two)
+        pairs.append(jnp.concatenate([left, right], axis=1))
     rows = shards * EX_DEV
     tests = half * TEX_DEV
     x = jnp.concatenate([train[...]] + pairs, axis=0)
@@ -217,7 +232,7 @@
         out_specs=VMEM,
         scratch_shapes=[
             pltpu.VMEM((shards * EX_DEV, 1024), F32),
-            pltpu.VMEM((shards, ROWS - EX_DEV, 1024), F32),
+            pltpu.VMEM((shards, EX_DEV, 512), F32),
         ],
         compiler_params=pltpu.CompilerParams(vmem_limit_bytes=16 << 20),
         name="scores",
@@ -228,9 +243,9 @@
     shards = lax.axis_size(("train", "test"))
     total = EX_DEV * shards
     everyone = lax.all_gather(own, ("train", "test"), axis=0)
-    width = own.shape[1]
-    train_full = everyone[:, :EX_DEV].reshape(total, width)
-    tests = everyone[:, EX_DEV : EX_DEV + TEX_DEV] + everyone[:, EX_DEV + TEX_DEV :]
+    width = 2 * own.shape[1] // 3
+    train_full = everyone[:, :, :width].reshape(total, width)
+    tests = jnp.concatenate([everyone[:, :TEX_DEV, width:], everyone[:, TEX_DEV:, width:]], axis=2)
     tests = tests.reshape(TEX_DEV * shards, width)
     cols = TEX_DEV * shards // lax.axis_size("proj")
     test_half = lax.dynamic_slice_in_dim(tests, lax.axis_index("proj") * cols, cols, 0)

time: 22.5 us -> 22 us (0.978)
  starting transfers between devices: 12.6 us -> 12 us
    ppermute x4, starting transfers between devices: 2.72 us -> 2.15 us  [body(): theirs = [lax.ppermute(x, 'proj', [(0, 1), (1, 0)]) for x in mine]]
where the time goes in v6:
time: 22 us; the launch traced here: 21.8 us
  starting transfers between devices  12 us (55%)
  Pallas kernels  7.31 us (33%)
  waiting for transfers between devices  2.38 us (11%)
    ppermute x4, starting transfers between devices, body(): mine.append(lax.ppermute(own, axes, route))  9.38 us
    pallas_call x1, Pallas kernels, project(): pl.pallas_call(project_kernel, out_shape=pltpu.VMEM((both, rin + rout), F...  3.45 us
    pallas_call x1, Pallas kernels, scores(): pl.pallas_call(functools.partial(score_kernel, routes, shards), out_shape...  2.92 us
    ppermute x4, starting transfers between devices, body(): theirs = [lax.ppermute(x, 'proj', [(0, 1), (1, 0)]) for x in mine]  2.15 us
    ppermute x4, waiting for transfers between devices, body(): theirs = [lax.ppermute(x, 'proj', [(0, 1), (1, 0)]) for x in mine]  1.22 us
    pallas_call x1, Pallas kernels, gradients(): pl.pallas_call(gradient_kernel, out_shape=jax.ShapeDtypeStruct((EX_DEV, 1...  0.94 us
    ppermute x1, waiting for transfers between devices, body(): other = lax.ppermute(part, 'proj', [(0, 1), (1, 0)])  0.94 us
    ppermute x1, starting transfers between devices, body(): other = lax.ppermute(part, 'proj', [(0, 1), (1, 0)])  0.52 us
  transfers between devices with their start and end apart: 9, of which 4 were waited for; matrix products, arithmetic and copies ran while one was open for 0% of the time, Pallas kernels for 0%

profile of v6, /device:TPU:0, one launch (start us, length us, event | category | flops | bytes accessed | tf_op | source)
XLA Modules:
  0.0 21.8 jit_solution(13069799683896304124)
XLA Ops:
  0.0 0.0 copy-start
  0.0 0.0 copy-start.1
  0.0 0.0 copy-start.2
  0.0 0.0 copy-start.3
  0.0 3.5 %project.1.own = f32[192,64]{1,0:T(8,128)S(1)} custom-call(bf16[128,2048]{1,0:T(8,128)(2,1)} %bitcast.8, bf16[128,7168]{1,0:T(8,128)(2,1)} %bitcast.6, bf16[64,2048]{1,0:T(8,128)(2,1)} %bitcast.10, bf16[64,7168]{1,0:T(8,128)(2,1)} %bitcast.7, bf16[32,2048]{1,0:T(8,128)(2,1)} %bitcast.11, bf16[32,7168]{1,0:T(8,128)(2,1)} %bitcast.9), custom_call_target="tpu_custom_call" | custom-call | tf_op jit(solution)/shard_map/project/pallas_call | solution.py:87
  3.5 0.5 %collective-permute-start = (f32[192,64]{1,0:T(8,128)S(1)}, f32[192,64]{1,0:T(8,128)S(1)}, u32[]{:S(2)}, u32[]{:S(2)}) collective-permute-start(f32[192,64]{1,0:T(8,128)S(1)} %project.1.own), channel_id=1, source_target_pairs={{0,1},{1,0},{2,3},{3,2},{4,5},{5,4},{6,7},{7,6},{8,9},{9,8},{10,11... | collective-permute-start | bytes 147464 | tf_op jit(solution)/shard_map/ppermute | solution.py:264
  4.0 0.9 %collective-permute-done.other = f32[192,64]{1,0:T(8,128)S(1)} collective-permute-done((f32[192,64]{1,0:T(8,128)S(1)}, f32[192,64]{1,0:T(8,128)S(1)}, u32[]{:S(2)}, u32[]{:S(2)}) %collective-permute-start) | collective-permute-done | bytes 49184 | tf_op jit(solution)/shard_map/ppermute | solution.py:264
  4.9 0.0 copy-done
  4.9 0.0 copy-done.1
  4.9 0.0 copy-done.2
  4.9 0.0 copy-done.3
  4.9 0.9 %gradients.1.own = f32[8,1536]{1,0:T(8,128)S(1)} custom-call(f32[192,64]{1,0:T(8,128)S(1)} %project.1.own, f32[192,64]{1,0:T(8,128)S(1)} %collective-permute-done.other, s32[1,128]{1,0:T(1,128)S(1)} %copy-done, s32[1,128]{1,0:T(1,128)S(1)} %copy-done.1, s32[1,64]{1,0:T(1,128)S(1)} %copy-done.2, s32[1,64]{1,0:T(1,128)S(1)} %copy-done.3), custom_call_target="tpu_custom_call" | custom-call | tf_op jit(solution)/shard_map/gradients/pallas_call | solution.py:138
  5.9 3.9 %collective-permute-start.4 = (f32[8,1536]{1,0:T(8,128)S(1)}, f32[8,1536]{1,0:T(8,128)S(1)}, u32[]{:S(2)}, u32[]{:S(2)}) collective-permute-start(f32[8,1536]{1,0:T(8,128)S(1)} %gradients.1.own), channel_id=1, source_target_pairs={{0,6},{2,4},{4,2},{6,0},{8,14},{10,12},{12,10},{14,8},{1,15},{3,13... | collective-permute-start | bytes 147464 | tf_op jit(solution)/shard_map/ppermute | solution.py:272
  9.8 0.4 %collective-permute-start.3 = (f32[8,1536]{1,0:T(8,128)S(1)}, f32[8,1536]{1,0:T(8,128)S(1)}, u32[]{:S(2)}, u32[]{:S(2)}) collective-permute-start(f32[8,1536]{1,0:T(8,128)S(1)} %gradients.1.own), channel_id=1, source_target_pairs={{0,4},{2,6},{4,0},{6,2},{8,12},{10,14},{12,8},{14,10},{1,13},{3,15... | collective-permute-start | bytes 147464 | tf_op jit(solution)/shard_map/ppermute | solution.py:272
  10.2 0.2 collective-permute-start.2
  10.4 4.8 %collective-permute-start.1 = (f32[8,1536]{1,0:T(8,128)S(1)}, f32[8,1536]{1,0:T(8,128)S(1)}, u32[]{:S(2)}, u32[]{:S(2)}) collective-permute-start(f32[8,1536]{1,0:T(8,128)S(1)} %gradients.1.own), channel_id=1, source_target_pairs={{0,8},{2,10},{4,12},{6,14},{8,0},{10,2},{12,4},{14,6},{16,24},{18,... | collective-permute-start | bytes 147464 | tf_op jit(solution)/shard_map/ppermute | solution.py:272
  15.3 0.0 collective-permute-done.4.refs_3_
  15.3 0.1 collective-permute-start.8
  15.4 0.0 collective-permute-done.3.refs_2_
  15.4 1.1 %collective-permute-start.7 = (f32[8,1536]{1,0:T(8,128)S(1)}, f32[8,1536]{1,0:T(8,128)S(1)}, u32[]{:S(2)}, u32[]{:S(2)}) collective-permute-start(f32[8,1536]{1,0:T(8,128)S(1)} %collective-permute-done.3.refs_2_), channel_id=1, source_target_pairs={{0,1},{1,0},{2,3},{3,2},{4,5},{5,4},{6,7},{7,6},{8,9},{9,8},{10,11... | collective-permute-start | bytes 147464 | tf_op jit(solution)/shard_map/ppermute | solution.py:273
  16.4 0.0 collective-permute-done.2.refs_1_
  16.4 1.0 %collective-permute-start.6 = (f32[8,1536]{1,0:T(8,128)S(1)}, f32[8,1536]{1,0:T(8,128)S(1)}, u32[]{:S(2)}, u32[]{:S(2)}) collective-permute-start(f32[8,1536]{1,0:T(8,128)S(1)} %collective-permute-done.2.refs_1_), channel_id=1, source_target_pairs={{0,1},{1,0},{2,3},{3,2},{4,5},{5,4},{6,7},{7,6},{8,9},{9,8},{10,11... | collective-permute-start | bytes 147464 | tf_op jit(solution)/shard_map/ppermute | solution.py:273
  17.5 0.2 collective-permute-done.1.refs_0_
  17.7 0.0 collective-permute-start.5
  17.7 0.0 collective-permute-done.8.refs_7_
  17.7 0.0 collective-permute-done.7.refs_6_
  17.7 0.7 %collective-permute-done.6.refs_5_ = f32[8,1536]{1,0:T(8,128)S(1)} collective-permute-done((f32[8,1536]{1,0:T(8,128)S(1)}, f32[8,1536]{1,0:T(8,128)S(1)}, u32[]{:S(2)}, u32[]{:S(2)}) %collective-permute-start.6) | collective-permute-done | bytes 49184 | tf_op jit(solution)/shard_map/ppermute | solution.py:273
  18.3 0.6 %collective-permute-done.5.refs_4_ = f32[8,1536]{1,0:T(8,128)S(1)} collective-permute-done((f32[8,1536]{1,0:T(8,128)S(1)}, f32[8,1536]{1,0:T(8,128)S(1)}, u32[]{:S(2)}, u32[]{:S(2)}) %collective-permute-start.5) | collective-permute-done | bytes 49184 | tf_op jit(solution)/shard_map/ppermute | solution.py:273
  18.9 2.9 %scores.1 = f32[8,16]{1,0:T(8,128)} custom-call(f32[8,1536]{1,0:T(8,128)S(1)} %gradients.1.own, f32[8,1536]{1,0:T(8,128)S(1)} %collective-permute-done.1.refs_0_, f32[8,1536]{1,0:T(8,128)S(1)} %collective-permute-done.2.refs_1_, f32[8,1536]{1,0:T(8,128)S(1)} %collective-permute-done.3.refs_2_, f32[8,1536]{1,0:T(8,128)S(1)} %collective-permute-done.4.refs_3_, ...), custom_call_target="tpu_custom_call" | custom-call | tf_op jit(solution)/shard_map/scores/pallas_call | solution.py:228
Async XLA Ops:
  0.0 4.9 %copy-start = (s32[1,128]{1,0:T(1,128)S(1)}, s32[1,128]{1,0:T(1,128)}, u32[]{:S(2)}) copy-start(s32[1,128]{1,0:T(1,128)} %tseg.1) | copy-start | bytes 1540
  0.0 4.9 %copy-start.1 = (s32[1,128]{1,0:T(1,128)S(1)}, s32[1,128]{1,0:T(1,128)}, u32[]{:S(2)}) copy-start(s32[1,128]{1,0:T(1,128)} %tmask.1) | copy-start | bytes 1540
  0.0 4.9 %copy-start.2 = (s32[1,64]{1,0:T(1,128)S(1)}, s32[1,64]{1,0:T(1,128)}, u32[]{:S(2)}) copy-start(s32[1,64]{1,0:T(1,128)} %sseg.1) | copy-start | bytes 772
  0.0 4.9 %copy-start.3 = (s32[1,64]{1,0:T(1,128)S(1)}, s32[1,64]{1,0:T(1,128)}, u32[]{:S(2)}) copy-start(s32[1,64]{1,0:T(1,128)} %smask.1) | copy-start | bytes 772
  3.5 1.5 %collective-permute-start = (f32[192,64]{1,0:T(8,128)S(1)}, f32[192,64]{1,0:T(8,128)S(1)}, u32[]{:S(2)}, u32[]{:S(2)}) collective-permute-start(f32[192,64]{1,0:T(8,128)S(1)} %project.1.own), channel_id=1, source_target_pairs={{0,1},{1,0},{2,3},{3,2},{4,5},{5,4},{6,7},{7,6},{8,9},{9,8},{10,11... | collective-permute-start | bytes 147464 | tf_op jit(solution)/shard_map/ppermute | solution.py:264
  5.9 9.4 %collective-permute-start.4 = (f32[8,1536]{1,0:T(8,128)S(1)}, f32[8,1536]{1,0:T(8,128)S(1)}, u32[]{:S(2)}, u32[]{:S(2)}) collective-permute-start(f32[8,1536]{1,0:T(8,128)S(1)} %gradients.1.own), channel_id=1, source_target_pairs={{0,6},{2,4},{4,2},{6,0},{8,14},{10,12},{12,10},{14,8},{1,15},{3,13... | collective-permute-start | bytes 147464 | tf_op jit(solution)/shard_map/ppermute | solution.py:272
  9.8 5.6 %collective-permute-start.3 = (f32[8,1536]{1,0:T(8,128)S(1)}, f32[8,1536]{1,0:T(8,128)S(1)}, u32[]{:S(2)}, u32[]{:S(2)}) collective-permute-start(f32[8,1536]{1,0:T(8,128)S(1)} %gradients.1.own), channel_id=1, source_target_pairs={{0,4},{2,6},{4,0},{6,2},{8,12},{10,14},{12,8},{14,10},{1,13},{3,15... | collective-permute-start | bytes 147464 | tf_op jit(solution)/shard_map/ppermute | solution.py:272
  10.2 6.2 %collective-permute-start.2 = (f32[8,1536]{1,0:T(8,128)S(1)}, f32[8,1536]{1,0:T(8,128)S(1)}, u32[]{:S(2)}, u32[]{:S(2)}) collective-permute-start(f32[8,1536]{1,0:T(8,128)S(1)} %gradients.1.own), channel_id=1, source_target_pairs={{0,2},{2,0},{4,6},{6,4},{8,10},{10,8},{12,14},{14,12},{1,11},{3,9}... | collective-permute-start | bytes 147464 | tf_op jit(solution)/shard_map/ppermute | solution.py:272
  10.4 7.2 %collective-permute-start.1 = (f32[8,1536]{1,0:T(8,128)S(1)}, f32[8,1536]{1,0:T(8,128)S(1)}, u32[]{:S(2)}, u32[]{:S(2)}) collective-permute-start(f32[8,1536]{1,0:T(8,128)S(1)} %gradients.1.own), channel_id=1, source_target_pairs={{0,8},{2,10},{4,12},{6,14},{8,0},{10,2},{12,4},{14,6},{16,24},{18,... | collective-permute-start | bytes 147464 | tf_op jit(solution)/shard_map/ppermute | solution.py:272
  15.3 2.4 %collective-permute-start.8 = (f32[8,1536]{1,0:T(8,128)S(1)}, f32[8,1536]{1,0:T(8,128)S(1)}, u32[]{:S(2)}, u32[]{:S(2)}) collective-permute-start(f32[8,1536]{1,0:T(8,128)S(1)} %collective-permute-done.4.refs_3_), channel_id=1, source_target_pairs={{0,1},{1,0},{2,3},{3,2},{4,5},{5,4},{6,7},{7,6},{8,9},{9,8},{10,11... | collective-permute-start | bytes 147464 | tf_op jit(solution)/shard_map/ppermute | solution.py:273
  15.4 2.3 %collective-permute-start.7 = (f32[8,1536]{1,0:T(8,128)S(1)}, f32[8,1536]{1,0:T(8,128)S(1)}, u32[]{:S(2)}, u32[]{:S(2)}) collective-permute-start(f32[8,1536]{1,0:T(8,128)S(1)} %collective-permute-done.3.refs_2_), channel_id=1, source_target_pairs={{0,1},{1,0},{2,3},{3,2},{4,5},{5,4},{6,7},{7,6},{8,9},{9,8},{10,11... | collective-permute-start | bytes 147464 | tf_op jit(solution)/shard_map/ppermute | solution.py:273
  16.4 1.9 %collective-permute-start.6 = (f32[8,1536]{1,0:T(8,128)S(1)}, f32[8,1536]{1,0:T(8,128)S(1)}, u32[]{:S(2)}, u32[]{:S(2)}) collective-permute-start(f32[8,1536]{1,0:T(8,128)S(1)} %collective-permute-done.2.refs_1_), channel_id=1, source_target_pairs={{0,1},{1,0},{2,3},{3,2},{4,5},{5,4},{6,7},{7,6},{8,9},{9,8},{10,11... | collective-permute-start | bytes 147464 | tf_op jit(solution)/shard_map/ppermute | solution.py:273
  17.7 1.2 %collective-permute-start.5 = (f32[8,1536]{1,0:T(8,128)S(1)}, f32[8,1536]{1,0:T(8,128)S(1)}, u32[]{:S(2)}, u32[]{:S(2)}) collective-permute-start(f32[8,1536]{1,0:T(8,128)S(1)} %collective-permute-done.1.refs_0_), channel_id=1, source_target_pairs={{0,1},{1,0},{2,3},{3,2},{4,5},{5,4},{6,7},{7,6},{8,9},{9,8},{10,11... | collective-permute-start | bytes 147464 | tf_op jit(solution)/shard_map/ppermute | solution.py:273

commit v7 on v6

--- a/solution.py
+++ b/solution.py
@@ -10,7 +10,7 @@
 EX_DEV = 8
 TEX_DEV = 4
 ROWS = 16
-ROUTES = ((4, 0), (1, 5), (2, 6), (3, 7))
+ROUTES = ((4, 4), (5, 1), (2, 6), (3, 7))
 F32 = jnp.float32
 BF16 = jnp.bfloat16
 NT = (((1,), (1,)), ((), ()))
@@ -176,10 +176,9 @@
 
 
 def score_kernel(routes, shards, own, *refs):
-    near = len(routes)
-    mine = refs[:near]
-    theirs = refs[near : 2 * near]
-    out, train, test = refs[2 * near :]
+    *blocks, out, train, test = refs
+    mine = blocks[: len(routes)]
+    theirs = iter(blocks[len(routes) :])
     shard, core = lax.axis_index(("train", "test")), lax.axis_index("proj")
 
     def put(block, mask):
@@ -189,7 +188,8 @@
 
     for k, (first, second) in enumerate(routes):
         put(mine[k], jnp.where(core == 0, first, second))
-        put(theirs[k], jnp.where(core == 0, second, first))
+        if first != second:
+            put(next(theirs), jnp.where(core == 0, second, first))
     put(own, 0)
 
     half = shards // 2
@@ -224,11 +224,11 @@
 
 
 def scores(own, mine, theirs, routes, shards):
-    near = len(mine)
+    blocks = (own, *mine, *theirs)
     return pl.pallas_call(
         functools.partial(score_kernel, routes, shards),
         out_shape=jax.ShapeDtypeStruct((EX_DEV, shards * TEX_DEV // 2), F32),
-        in_specs=[VMEM] * (1 + 2 * near),
+        in_specs=[VMEM] * len(blocks),
         out_specs=VMEM,
         scratch_shapes=[
             pltpu.VMEM((shards * EX_DEV, 1024), F32),
@@ -236,7 +236,7 @@
         ],
         compiler_params=pltpu.CompilerParams(vmem_limit_bytes=16 << 20),
         name="scores",
-    )(own, *mine, *theirs)
+    )(*blocks)
 
 
 def large(own):
@@ -268,9 +268,9 @@
     axes = ("train", "test", "proj")
     mine = []
     for pair in ROUTES:
-        route = [(2 * i + c, 2 * (i ^ pair[c]) + c) for c in range(2) if pair[c] for i in range(shards)]
+        route = [(2 * i + c, 2 * (i ^ pair[c]) + c) for c in range(2) for i in range(shards)]
         mine.append(lax.ppermute(own, axes, route))
-    theirs = [lax.ppermute(x, "proj", [(0, 1), (1, 0)]) for x in mine]
+    theirs = [lax.ppermute(x, "proj", [(0, 1), (1, 0)]) for x, pair in zip(mine, ROUTES) if pair[0] != pair[1]]
     return scores(own, mine, theirs, ROUTES, shards)
 
 

time: 22 us -> 21.3 us (0.968)
  starting transfers between devices: 12 us -> 10.8 us
  waiting for transfers between devices: 2.38 us -> 2.95 us
    ppermute x4, starting transfers between devices: 9.38 us -> 6.95 us  [body(): mine.append(lax.ppermute(own, axes, route))]
    ppermute x4, waiting for transfers between devices: 0.21 us -> 2 us  [body(): mine.append(lax.ppermute(own, axes, route))]
    ppermute x4 -> x3, waiting for transfers between devices: 1.22 us -> 0.01 us  [body(): lax.ppermute(x, 'proj', [(0, 1), (1, 0)])]
    ppermute x4 -> x3, starting transfers between devices: 2.15 us -> 3.34 us  [body(): lax.ppermute(x, 'proj', [(0, 1), (1, 0)])]
  transfers between devices with their start and end apart: 9 -> 8, of which waited for: 4 -> 3; matrix products, arithmetic and copies ran while one was open for 0% -> 0% of each run, Pallas kernels for 0% -> 0%
where the time goes in v7:
time: 21.3 us; the launch traced here: 21.1 us
  starting transfers between devices  10.8 us (51%)
  Pallas kernels  7.32 us (34%)
  waiting for transfers between devices  2.95 us (14%)
    ppermute x4, starting transfers between devices, body(): mine.append(lax.ppermute(own, axes, route))  6.95 us
    pallas_call x1, Pallas kernels, project(): pl.pallas_call(project_kernel, out_shape=pltpu.VMEM((both, rin + rout), F...  3.45 us
    ppermute x3, starting transfers between devices, body(): lax.ppermute(x, 'proj', [(0, 1), (1, 0)])  3.34 us
    pallas_call x1, Pallas kernels, scores(): pl.pallas_call(functools.partial(score_kernel, routes, shards), out_shape...  2.93 us
    ppermute x4, waiting for transfers between devices, body(): mine.append(lax.ppermute(own, axes, route))  2 us
    pallas_call x1, Pallas kernels, gradients(): pl.pallas_call(gradient_kernel, out_shape=jax.ShapeDtypeStruct((EX_DEV, 1...  0.94 us
    ppermute x1, waiting for transfers between devices, body(): other = lax.ppermute(part, 'proj', [(0, 1), (1, 0)])  0.94 us
    ppermute x1, starting transfers between devices, body(): other = lax.ppermute(part, 'proj', [(0, 1), (1, 0)])  0.52 us
  transfers between devices with their start and end apart: 8, of which 3 were waited for; matrix products, arithmetic and copies ran while one was open for 0% of the time, Pallas kernels for 0%

profile of v7, /device:TPU:0, one launch (start us, length us, event | category | flops | bytes accessed | tf_op | source)
XLA Modules:
  0.0 21.1 jit_solution(3123219882395765017)
XLA Ops:
  0.0 0.0 copy-start
  0.0 0.0 copy-start.1
  0.0 0.0 copy-start.2
  0.0 0.0 copy-start.3
  0.0 3.5 %project.1.own = f32[192,64]{1,0:T(8,128)S(1)} custom-call(bf16[128,2048]{1,0:T(8,128)(2,1)} %bitcast.8, bf16[128,7168]{1,0:T(8,128)(2,1)} %bitcast.6, bf16[64,2048]{1,0:T(8,128)(2,1)} %bitcast.10, bf16[64,7168]{1,0:T(8,128)(2,1)} %bitcast.7, bf16[32,2048]{1,0:T(8,128)(2,1)} %bitcast.11, bf16[32,7168]{1,0:T(8,128)(2,1)} %bitcast.9), custom_call_target="tpu_custom_call" | custom-call | tf_op jit(solution)/shard_map/project/pallas_call | solution.py:87
  3.5 0.5 %collective-permute-start = (f32[192,64]{1,0:T(8,128)S(1)}, f32[192,64]{1,0:T(8,128)S(1)}, u32[]{:S(2)}, u32[]{:S(2)}) collective-permute-start(f32[192,64]{1,0:T(8,128)S(1)} %project.1.own), channel_id=1, source_target_pairs={{0,1},{1,0},{2,3},{3,2},{4,5},{5,4},{6,7},{7,6},{8,9},{9,8},{10,11... | collective-permute-start | bytes 147464 | tf_op jit(solution)/shard_map/ppermute | solution.py:264
  4.0 0.9 %collective-permute-done.other = f32[192,64]{1,0:T(8,128)S(1)} collective-permute-done((f32[192,64]{1,0:T(8,128)S(1)}, f32[192,64]{1,0:T(8,128)S(1)}, u32[]{:S(2)}, u32[]{:S(2)}) %collective-permute-start) | collective-permute-done | bytes 49184 | tf_op jit(solution)/shard_map/ppermute | solution.py:264
  4.9 0.0 copy-done
  4.9 0.0 copy-done.1
  4.9 0.0 copy-done.2
  4.9 0.0 copy-done.3
  4.9 0.9 %gradients.1.own = f32[8,1536]{1,0:T(8,128)S(1)} custom-call(f32[192,64]{1,0:T(8,128)S(1)} %project.1.own, f32[192,64]{1,0:T(8,128)S(1)} %collective-permute-done.other, s32[1,128]{1,0:T(1,128)S(1)} %copy-done, s32[1,128]{1,0:T(1,128)S(1)} %copy-done.1, s32[1,64]{1,0:T(1,128)S(1)} %copy-done.2, s32[1,64]{1,0:T(1,128)S(1)} %copy-done.3), custom_call_target="tpu_custom_call" | custom-call | tf_op jit(solution)/shard_map/gradients/pallas_call | solution.py:138
  5.9 3.9 %collective-permute-start.4 = (f32[8,1536]{1,0:T(8,128)S(1)}, f32[8,1536]{1,0:T(8,128)S(1)}, u32[]{:S(2)}, u32[]{:S(2)}) collective-permute-start(f32[8,1536]{1,0:T(8,128)S(1)} %gradients.1.own), channel_id=1, source_target_pairs={{0,6},{2,4},{4,2},{6,0},{8,14},{10,12},{12,10},{14,8},{1,15},{3,13... | collective-permute-start | bytes 147464 | tf_op jit(solution)/shard_map/ppermute | solution.py:272
  9.8 0.4 %collective-permute-start.3 = (f32[8,1536]{1,0:T(8,128)S(1)}, f32[8,1536]{1,0:T(8,128)S(1)}, u32[]{:S(2)}, u32[]{:S(2)}) collective-permute-start(f32[8,1536]{1,0:T(8,128)S(1)} %gradients.1.own), channel_id=1, source_target_pairs={{0,4},{2,6},{4,0},{6,2},{8,12},{10,14},{12,8},{14,10},{1,13},{3,15... | collective-permute-start | bytes 147464 | tf_op jit(solution)/shard_map/ppermute | solution.py:272
  10.2 2.6 %collective-permute-start.2 = (f32[8,1536]{1,0:T(8,128)S(1)}, f32[8,1536]{1,0:T(8,128)S(1)}, u32[]{:S(2)}, u32[]{:S(2)}) collective-permute-start(f32[8,1536]{1,0:T(8,128)S(1)} %gradients.1.own), channel_id=1, source_target_pairs={{0,10},{2,8},{4,14},{6,12},{8,2},{10,0},{12,6},{14,4},{1,3},{3,1},... | collective-permute-start | bytes 147464 | tf_op jit(solution)/shard_map/ppermute | solution.py:272
  12.8 0.0 collective-permute-start.1
  12.8 0.0 collective-permute-done.4.refs_3_
  12.8 0.3 %collective-permute-start.7 = (f32[8,1536]{1,0:T(8,128)S(1)}, f32[8,1536]{1,0:T(8,128)S(1)}, u32[]{:S(2)}, u32[]{:S(2)}) collective-permute-start(f32[8,1536]{1,0:T(8,128)S(1)} %collective-permute-done.4.refs_3_), channel_id=1, source_target_pairs={{0,1},{1,0},{2,3},{3,2},{4,5},{5,4},{6,7},{7,6},{8,9},{9,8},{10,11... | collective-permute-start | bytes 147464 | tf_op jit(solution)/shard_map/ppermute | solution.py:273
  13.2 0.7 %collective-permute-done.3.refs_2_ = f32[8,1536]{1,0:T(8,128)S(1)} collective-permute-done((f32[8,1536]{1,0:T(8,128)S(1)}, f32[8,1536]{1,0:T(8,128)S(1)}, u32[]{:S(2)}, u32[]{:S(2)}) %collective-permute-start.3) | collective-permute-done | bytes 49184 | tf_op jit(solution)/shard_map/ppermute | solution.py:272
  13.9 3.0 %collective-permute-start.6 = (f32[8,1536]{1,0:T(8,128)S(1)}, f32[8,1536]{1,0:T(8,128)S(1)}, u32[]{:S(2)}, u32[]{:S(2)}) collective-permute-start(f32[8,1536]{1,0:T(8,128)S(1)} %collective-permute-done.3.refs_2_), channel_id=1, source_target_pairs={{0,1},{1,0},{2,3},{3,2},{4,5},{5,4},{6,7},{7,6},{8,9},{9,8},{10,11... | collective-permute-start | bytes 147464 | tf_op jit(solution)/shard_map/ppermute | solution.py:273
  16.9 0.0 collective-permute-done.2.refs_1_
  16.9 0.0 collective-permute-start.5
  16.9 1.3 %collective-permute-done.1.refs_0_ = f32[8,1536]{1,0:T(8,128)S(1)} collective-permute-done((f32[8,1536]{1,0:T(8,128)S(1)}, f32[8,1536]{1,0:T(8,128)S(1)}, u32[]{:S(2)}, u32[]{:S(2)}) %collective-permute-start.1) | collective-permute-done | bytes 49184 | tf_op jit(solution)/shard_map/ppermute | solution.py:272
  18.2 0.0 collective-permute-done.7.refs_6_
  18.2 0.0 collective-permute-done.6.refs_5_
  18.2 0.0 collective-permute-done.5.refs_4_
  18.2 2.9 %scores.1 = f32[8,16]{1,0:T(8,128)} custom-call(f32[8,1536]{1,0:T(8,128)S(1)} %gradients.1.own, f32[8,1536]{1,0:T(8,128)S(1)} %collective-permute-done.1.refs_0_, f32[8,1536]{1,0:T(8,128)S(1)} %collective-permute-done.2.refs_1_, f32[8,1536]{1,0:T(8,128)S(1)} %collective-permute-done.3.refs_2_, f32[8,1536]{1,0:T(8,128)S(1)} %collective-permute-done.4.refs_3_, ...), custom_call_target="tpu_custom_call" | custom-call | tf_op jit(solution)/shard_map/scores/pallas_call | solution.py:228
Async XLA Ops:
  0.0 4.9 %copy-start = (s32[1,128]{1,0:T(1,128)S(1)}, s32[1,128]{1,0:T(1,128)}, u32[]{:S(2)}) copy-start(s32[1,128]{1,0:T(1,128)} %tseg.1) | copy-start | bytes 1540
  0.0 4.9 %copy-start.1 = (s32[1,128]{1,0:T(1,128)S(1)}, s32[1,128]{1,0:T(1,128)}, u32[]{:S(2)}) copy-start(s32[1,128]{1,0:T(1,128)} %tmask.1) | copy-start | bytes 1540
  0.0 4.9 %copy-start.2 = (s32[1,64]{1,0:T(1,128)S(1)}, s32[1,64]{1,0:T(1,128)}, u32[]{:S(2)}) copy-start(s32[1,64]{1,0:T(1,128)} %sseg.1) | copy-start | bytes 772
  0.0 4.9 %copy-start.3 = (s32[1,64]{1,0:T(1,128)S(1)}, s32[1,64]{1,0:T(1,128)}, u32[]{:S(2)}) copy-start(s32[1,64]{1,0:T(1,128)} %smask.1) | copy-start | bytes 772
  3.5 1.5 %collective-permute-start = (f32[192,64]{1,0:T(8,128)S(1)}, f32[192,64]{1,0:T(8,128)S(1)}, u32[]{:S(2)}, u32[]{:S(2)}) collective-permute-start(f32[192,64]{1,0:T(8,128)S(1)} %project.1.own), channel_id=1, source_target_pairs={{0,1},{1,0},{2,3},{3,2},{4,5},{5,4},{6,7},{7,6},{8,9},{9,8},{10,11... | collective-permute-start | bytes 147464 | tf_op jit(solution)/shard_map/ppermute | solution.py:264
  5.9 7.0 %collective-permute-start.4 = (f32[8,1536]{1,0:T(8,128)S(1)}, f32[8,1536]{1,0:T(8,128)S(1)}, u32[]{:S(2)}, u32[]{:S(2)}) collective-permute-start(f32[8,1536]{1,0:T(8,128)S(1)} %gradients.1.own), channel_id=1, source_target_pairs={{0,6},{2,4},{4,2},{6,0},{8,14},{10,12},{12,10},{14,8},{1,15},{3,13... | collective-permute-start | bytes 147464 | tf_op jit(solution)/shard_map/ppermute | solution.py:272
  9.8 4.1 %collective-permute-start.3 = (f32[8,1536]{1,0:T(8,128)S(1)}, f32[8,1536]{1,0:T(8,128)S(1)}, u32[]{:S(2)}, u32[]{:S(2)}) collective-permute-start(f32[8,1536]{1,0:T(8,128)S(1)} %gradients.1.own), channel_id=1, source_target_pairs={{0,4},{2,6},{4,0},{6,2},{8,12},{10,14},{12,8},{14,10},{1,13},{3,15... | collective-permute-start | bytes 147464 | tf_op jit(solution)/shard_map/ppermute | solution.py:272
  10.2 6.6 %collective-permute-start.2 = (f32[8,1536]{1,0:T(8,128)S(1)}, f32[8,1536]{1,0:T(8,128)S(1)}, u32[]{:S(2)}, u32[]{:S(2)}) collective-permute-start(f32[8,1536]{1,0:T(8,128)S(1)} %gradients.1.own), channel_id=1, source_target_pairs={{0,10},{2,8},{4,14},{6,12},{8,2},{10,0},{12,6},{14,4},{1,3},{3,1},... | collective-permute-start | bytes 147464 | tf_op jit(solution)/shard_map/ppermute | solution.py:272
  12.8 5.4 %collective-permute-start.1 = (f32[8,1536]{1,0:T(8,128)S(1)}, f32[8,1536]{1,0:T(8,128)S(1)}, u32[]{:S(2)}, u32[]{:S(2)}) collective-permute-start(f32[8,1536]{1,0:T(8,128)S(1)} %gradients.1.own), channel_id=1, source_target_pairs={{0,8},{2,10},{4,12},{6,14},{8,0},{10,2},{12,4},{14,6},{1,9},{3,11}... | collective-permute-start | bytes 147464 | tf_op jit(solution)/shard_map/ppermute | solution.py:272
  12.8 5.3 %collective-permute-start.7 = (f32[8,1536]{1,0:T(8,128)S(1)}, f32[8,1536]{1,0:T(8,128)S(1)}, u32[]{:S(2)}, u32[]{:S(2)}) collective-permute-start(f32[8,1536]{1,0:T(8,128)S(1)} %collective-permute-done.4.refs_3_), channel_id=1, source_target_pairs={{0,1},{1,0},{2,3},{3,2},{4,5},{5,4},{6,7},{7,6},{8,9},{9,8},{10,11... | collective-permute-start | bytes 147464 | tf_op jit(solution)/shard_map/ppermute | solution.py:273
  13.9 4.3 %collective-permute-start.6 = (f32[8,1536]{1,0:T(8,128)S(1)}, f32[8,1536]{1,0:T(8,128)S(1)}, u32[]{:S(2)}, u32[]{:S(2)}) collective-permute-start(f32[8,1536]{1,0:T(8,128)S(1)} %collective-permute-done.3.refs_2_), channel_id=1, source_target_pairs={{0,1},{1,0},{2,3},{3,2},{4,5},{5,4},{6,7},{7,6},{8,9},{9,8},{10,11... | collective-permute-start | bytes 147464 | tf_op jit(solution)/shard_map/ppermute | solution.py:273
  16.9 1.3 %collective-permute-start.5 = (f32[8,1536]{1,0:T(8,128)S(1)}, f32[8,1536]{1,0:T(8,128)S(1)}, u32[]{:S(2)}, u32[]{:S(2)}) collective-permute-start(f32[8,1536]{1,0:T(8,128)S(1)} %collective-permute-done.2.refs_1_), channel_id=1, source_target_pairs={{0,1},{1,0},{2,3},{3,2},{4,5},{5,4},{6,7},{7,6},{8,9},{9,8},{10,11... | collective-permute-start | bytes 147464 | tf_op jit(solution)/shard_map/ppermute | solution.py:273

commit v8 on v7

--- a/solution.py
+++ b/solution.py
@@ -55,7 +55,7 @@
         copy(pout, wout),
     ]
     later = []
-    for start, size in chunks_of(grads.shape[1], 4):
+    for start, size in chunks_of(grads.shape[1], 2):
         cols = pl.ds(start, size)
         later.append(
             (
@@ -112,8 +112,8 @@
     spread_x = (row == col // rout).astype(BF16)
     spread_g = (row - rin == col[:, :] % rout).astype(BF16)
     parts = split(full)
-    xrep = sum(mm(part, spread_x, NN) for part in parts[::-1])
-    grep = sum(mm(part, spread_g[:, :128], NN) for part in parts[::-1])
+    xrep = sum(mm(part, spread_x, NN) for part in parts[1::-1])
+    grep = sum(mm(part, spread_g[:, :128], NN) for part in parts[1::-1])
     tokens = tseg.shape[1]
     keep = jnp.concatenate([tmask[...], smask[...]], axis=1)
     ex = lax.broadcasted_iota(jnp.int32, (ROWS, both), 0)
@@ -126,7 +126,7 @@
     for start in range(0, width, 128):
         outer = xrep[:, start : start + 128] * grep
         side, place = divmod(start, half)
-        total = sum(mm(weights[side], part, NN) for part in split(outer)[::-1])
+        total = sum(mm(weights[side], part, NN) for part in split(outer)[1::-1])
         out[:, start : start + 128] = total[:EX_DEV]
         if side == 0:
             upper[place] = total[EX_DEV:]

time: 21.3 us -> 21 us (0.986)
  Pallas kernels: 7.32 us -> 7.05 us
    pallas_call x1, Pallas kernels: 0.94 us -> 0.69 us  [gradients(): pl.pallas_call(gradient_kernel, out_shape=jax.ShapeDtypeStruct((EX_DEV, 1...]
where the time goes in v8:
time: 21 us; the launch traced here: 20.9 us
  starting transfers between devices  10.8 us (51%)
  Pallas kernels  7.05 us (34%)
  waiting for transfers between devices  2.95 us (14%)
    ppermute x4, starting transfers between devices, body(): mine.append(lax.ppermute(own, axes, route))  6.97 us
    pallas_call x1, Pallas kernels, project(): pl.pallas_call(project_kernel, out_shape=pltpu.VMEM((both, rin + rout), F...  3.43 us
    ppermute x3, starting transfers between devices, body(): lax.ppermute(x, 'proj', [(0, 1), (1, 0)])  3.33 us
    pallas_call x1, Pallas kernels, scores(): pl.pallas_call(functools.partial(score_kernel, routes, shards), out_shape...  2.93 us
    ppermute x4, waiting for transfers between devices, body(): mine.append(lax.ppermute(own, axes, route))  2 us
    ppermute x1, waiting for transfers between devices, body(): other = lax.ppermute(part, 'proj', [(0, 1), (1, 0)])  0.94 us
    pallas_call x1, Pallas kernels, gradients(): pl.pallas_call(gradient_kernel, out_shape=jax.ShapeDtypeStruct((EX_DEV, 1...  0.69 us
    ppermute x1, starting transfers between devices, body(): other = lax.ppermute(part, 'proj', [(0, 1), (1, 0)])  0.51 us
  transfers between devices with their start and end apart: 8, of which 3 were waited for; matrix products, arithmetic and copies ran while one was open for 0% of the time, Pallas kernels for 0%

profile of v8, /device:TPU:0, one launch (start us, length us, event | category | flops | bytes accessed | tf_op | source)
XLA Modules:
  0.0 20.9 jit_solution(13872175611559806715)
XLA Ops:
  0.0 0.0 copy-start
  0.0 0.0 copy-start.1
  0.0 0.0 copy-start.2
  0.0 0.0 copy-start.3
  0.0 3.4 %project.1.own = f32[192,64]{1,0:T(8,128)S(1)} custom-call(bf16[128,2048]{1,0:T(8,128)(2,1)} %bitcast.8, bf16[128,7168]{1,0:T(8,128)(2,1)} %bitcast.6, bf16[64,2048]{1,0:T(8,128)(2,1)} %bitcast.10, bf16[64,7168]{1,0:T(8,128)(2,1)} %bitcast.7, bf16[32,2048]{1,0:T(8,128)(2,1)} %bitcast.11, bf16[32,7168]{1,0:T(8,128)(2,1)} %bitcast.9), custom_call_target="tpu_custom_call" | custom-call | tf_op jit(solution)/shard_map/project/pallas_call | solution.py:87
  3.4 0.5 %collective-permute-start = (f32[192,64]{1,0:T(8,128)S(1)}, f32[192,64]{1,0:T(8,128)S(1)}, u32[]{:S(2)}, u32[]{:S(2)}) collective-permute-start(f32[192,64]{1,0:T(8,128)S(1)} %project.1.own), channel_id=1, source_target_pairs={{0,1},{1,0},{2,3},{3,2},{4,5},{5,4},{6,7},{7,6},{8,9},{9,8},{10,11... | collective-permute-start | bytes 147464 | tf_op jit(solution)/shard_map/ppermute | solution.py:264
  4.0 0.9 %collective-permute-done.other = f32[192,64]{1,0:T(8,128)S(1)} collective-permute-done((f32[192,64]{1,0:T(8,128)S(1)}, f32[192,64]{1,0:T(8,128)S(1)}, u32[]{:S(2)}, u32[]{:S(2)}) %collective-permute-start) | collective-permute-done | bytes 49184 | tf_op jit(solution)/shard_map/ppermute | solution.py:264
  4.9 0.0 copy-done
  4.9 0.0 copy-done.1
  4.9 0.0 copy-done.2
  4.9 0.0 copy-done.3
  4.9 0.7 %gradients.1.own = f32[8,1536]{1,0:T(8,128)S(1)} custom-call(f32[192,64]{1,0:T(8,128)S(1)} %project.1.own, f32[192,64]{1,0:T(8,128)S(1)} %collective-permute-done.other, s32[1,128]{1,0:T(1,128)S(1)} %copy-done, s32[1,128]{1,0:T(1,128)S(1)} %copy-done.1, s32[1,64]{1,0:T(1,128)S(1)} %copy-done.2, s32[1,64]{1,0:T(1,128)S(1)} %copy-done.3), custom_call_target="tpu_custom_call" | custom-call | tf_op jit(solution)/shard_map/gradients/pallas_call | solution.py:138
  5.6 3.9 %collective-permute-start.4 = (f32[8,1536]{1,0:T(8,128)S(1)}, f32[8,1536]{1,0:T(8,128)S(1)}, u32[]{:S(2)}, u32[]{:S(2)}) collective-permute-start(f32[8,1536]{1,0:T(8,128)S(1)} %gradients.1.own), channel_id=1, source_target_pairs={{0,6},{2,4},{4,2},{6,0},{8,14},{10,12},{12,10},{14,8},{1,15},{3,13... | collective-permute-start | bytes 147464 | tf_op jit(solution)/shard_map/ppermute | solution.py:272
  9.5 0.4 %collective-permute-start.3 = (f32[8,1536]{1,0:T(8,128)S(1)}, f32[8,1536]{1,0:T(8,128)S(1)}, u32[]{:S(2)}, u32[]{:S(2)}) collective-permute-start(f32[8,1536]{1,0:T(8,128)S(1)} %gradients.1.own), channel_id=1, source_target_pairs={{0,4},{2,6},{4,0},{6,2},{8,12},{10,14},{12,8},{14,10},{1,13},{3,15... | collective-permute-start | bytes 147464 | tf_op jit(solution)/shard_map/ppermute | solution.py:272
  10.0 2.6 %collective-permute-start.2 = (f32[8,1536]{1,0:T(8,128)S(1)}, f32[8,1536]{1,0:T(8,128)S(1)}, u32[]{:S(2)}, u32[]{:S(2)}) collective-permute-start(f32[8,1536]{1,0:T(8,128)S(1)} %gradients.1.own), channel_id=1, source_target_pairs={{0,10},{2,8},{4,14},{6,12},{8,2},{10,0},{12,6},{14,4},{1,3},{3,1},... | collective-permute-start | bytes 147464 | tf_op jit(solution)/shard_map/ppermute | solution.py:272
  12.6 0.0 collective-permute-start.1
  12.6 0.0 collective-permute-done.4.refs_3_
  12.6 0.3 %collective-permute-start.7 = (f32[8,1536]{1,0:T(8,128)S(1)}, f32[8,1536]{1,0:T(8,128)S(1)}, u32[]{:S(2)}, u32[]{:S(2)}) collective-permute-start(f32[8,1536]{1,0:T(8,128)S(1)} %collective-permute-done.4.refs_3_), channel_id=1, source_target_pairs={{0,1},{1,0},{2,3},{3,2},{4,5},{5,4},{6,7},{7,6},{8,9},{9,8},{10,11... | collective-permute-start | bytes 147464 | tf_op jit(solution)/shard_map/ppermute | solution.py:273
  12.9 0.7 %collective-permute-done.3.refs_2_ = f32[8,1536]{1,0:T(8,128)S(1)} collective-permute-done((f32[8,1536]{1,0:T(8,128)S(1)}, f32[8,1536]{1,0:T(8,128)S(1)}, u32[]{:S(2)}, u32[]{:S(2)}) %collective-permute-start.3) | collective-permute-done | bytes 49184 | tf_op jit(solution)/shard_map/ppermute | solution.py:272
  13.6 3.0 %collective-permute-start.6 = (f32[8,1536]{1,0:T(8,128)S(1)}, f32[8,1536]{1,0:T(8,128)S(1)}, u32[]{:S(2)}, u32[]{:S(2)}) collective-permute-start(f32[8,1536]{1,0:T(8,128)S(1)} %collective-permute-done.3.refs_2_), channel_id=1, source_target_pairs={{0,1},{1,0},{2,3},{3,2},{4,5},{5,4},{6,7},{7,6},{8,9},{9,8},{10,11... | collective-permute-start | bytes 147464 | tf_op jit(solution)/shard_map/ppermute | solution.py:273
  16.6 0.0 collective-permute-done.2.refs_1_
  16.6 0.0 collective-permute-start.5
  16.6 1.3 %collective-permute-done.1.refs_0_ = f32[8,1536]{1,0:T(8,128)S(1)} collective-permute-done((f32[8,1536]{1,0:T(8,128)S(1)}, f32[8,1536]{1,0:T(8,128)S(1)}, u32[]{:S(2)}, u32[]{:S(2)}) %collective-permute-start.1) | collective-permute-done | bytes 49184 | tf_op jit(solution)/shard_map/ppermute | solution.py:272
  17.9 0.0 collective-permute-done.7.refs_6_
  17.9 0.0 collective-permute-done.6.refs_5_
  17.9 0.0 collective-permute-done.5.refs_4_
  17.9 2.9 %scores.1 = f32[8,16]{1,0:T(8,128)} custom-call(f32[8,1536]{1,0:T(8,128)S(1)} %gradients.1.own, f32[8,1536]{1,0:T(8,128)S(1)} %collective-permute-done.1.refs_0_, f32[8,1536]{1,0:T(8,128)S(1)} %collective-permute-done.2.refs_1_, f32[8,1536]{1,0:T(8,128)S(1)} %collective-permute-done.3.refs_2_, f32[8,1536]{1,0:T(8,128)S(1)} %collective-permute-done.4.refs_3_, ...), custom_call_target="tpu_custom_call" | custom-call | tf_op jit(solution)/shard_map/scores/pallas_call | solution.py:228
Async XLA Ops:
  0.0 4.9 %copy-start = (s32[1,128]{1,0:T(1,128)S(1)}, s32[1,128]{1,0:T(1,128)}, u32[]{:S(2)}) copy-start(s32[1,128]{1,0:T(1,128)} %tseg.1) | copy-start | bytes 1540
  0.0 4.9 %copy-start.1 = (s32[1,128]{1,0:T(1,128)S(1)}, s32[1,128]{1,0:T(1,128)}, u32[]{:S(2)}) copy-start(s32[1,128]{1,0:T(1,128)} %tmask.1) | copy-start | bytes 1540
  0.0 4.9 %copy-start.2 = (s32[1,64]{1,0:T(1,128)S(1)}, s32[1,64]{1,0:T(1,128)}, u32[]{:S(2)}) copy-start(s32[1,64]{1,0:T(1,128)} %sseg.1) | copy-start | bytes 772
  0.0 4.9 %copy-start.3 = (s32[1,64]{1,0:T(1,128)S(1)}, s32[1,64]{1,0:T(1,128)}, u32[]{:S(2)}) copy-start(s32[1,64]{1,0:T(1,128)} %smask.1) | copy-start | bytes 772
  3.4 1.5 %collective-permute-start = (f32[192,64]{1,0:T(8,128)S(1)}, f32[192,64]{1,0:T(8,128)S(1)}, u32[]{:S(2)}, u32[]{:S(2)}) collective-permute-start(f32[192,64]{1,0:T(8,128)S(1)} %project.1.own), channel_id=1, source_target_pairs={{0,1},{1,0},{2,3},{3,2},{4,5},{5,4},{6,7},{7,6},{8,9},{9,8},{10,11... | collective-permute-start | bytes 147464 | tf_op jit(solution)/shard_map/ppermute | solution.py:264
  5.6 7.0 %collective-permute-start.4 = (f32[8,1536]{1,0:T(8,128)S(1)}, f32[8,1536]{1,0:T(8,128)S(1)}, u32[]{:S(2)}, u32[]{:S(2)}) collective-permute-start(f32[8,1536]{1,0:T(8,128)S(1)} %gradients.1.own), channel_id=1, source_target_pairs={{0,6},{2,4},{4,2},{6,0},{8,14},{10,12},{12,10},{14,8},{1,15},{3,13... | collective-permute-start | bytes 147464 | tf_op jit(solution)/shard_map/ppermute | solution.py:272
  9.5 4.1 %collective-permute-start.3 = (f32[8,1536]{1,0:T(8,128)S(1)}, f32[8,1536]{1,0:T(8,128)S(1)}, u32[]{:S(2)}, u32[]{:S(2)}) collective-permute-start(f32[8,1536]{1,0:T(8,128)S(1)} %gradients.1.own), channel_id=1, source_target_pairs={{0,4},{2,6},{4,0},{6,2},{8,12},{10,14},{12,8},{14,10},{1,13},{3,15... | collective-permute-start | bytes 147464 | tf_op jit(solution)/shard_map/ppermute | solution.py:272
  10.0 6.6 %collective-permute-start.2 = (f32[8,1536]{1,0:T(8,128)S(1)}, f32[8,1536]{1,0:T(8,128)S(1)}, u32[]{:S(2)}, u32[]{:S(2)}) collective-permute-start(f32[8,1536]{1,0:T(8,128)S(1)} %gradients.1.own), channel_id=1, source_target_pairs={{0,10},{2,8},{4,14},{6,12},{8,2},{10,0},{12,6},{14,4},{1,3},{3,1},... | collective-permute-start | bytes 147464 | tf_op jit(solution)/shard_map/ppermute | solution.py:272
  12.6 5.4 %collective-permute-start.1 = (f32[8,1536]{1,0:T(8,128)S(1)}, f32[8,1536]{1,0:T(8,128)S(1)}, u32[]{:S(2)}, u32[]{:S(2)}) collective-permute-start(f32[8,1536]{1,0:T(8,128)S(1)} %gradients.1.own), channel_id=1, source_target_pairs={{0,8},{2,10},{4,12},{6,14},{8,0},{10,2},{12,4},{14,6},{1,9},{3,11}... | collective-permute-start | bytes 147464 | tf_op jit(solution)/shard_map/ppermute | solution.py:272
  12.6 5.3 %collective-permute-start.7 = (f32[8,1536]{1,0:T(8,128)S(1)}, f32[8,1536]{1,0:T(8,128)S(1)}, u32[]{:S(2)}, u32[]{:S(2)}) collective-permute-start(f32[8,1536]{1,0:T(8,128)S(1)} %collective-permute-done.4.refs_3_), channel_id=1, source_target_pairs={{0,1},{1,0},{2,3},{3,2},{4,5},{5,4},{6,7},{7,6},{8,9},{9,8},{10,11... | collective-permute-start | bytes 147464 | tf_op jit(solution)/shard_map/ppermute | solution.py:273
  13.6 4.3 %collective-permute-start.6 = (f32[8,1536]{1,0:T(8,128)S(1)}, f32[8,1536]{1,0:T(8,128)S(1)}, u32[]{:S(2)}, u32[]{:S(2)}) collective-permute-start(f32[8,1536]{1,0:T(8,128)S(1)} %collective-permute-done.3.refs_2_), channel_id=1, source_target_pairs={{0,1},{1,0},{2,3},{3,2},{4,5},{5,4},{6,7},{7,6},{8,9},{9,8},{10,11... | collective-permute-start | bytes 147464 | tf_op jit(solution)/shard_map/ppermute | solution.py:273
  16.6 1.3 %collective-permute-start.5 = (f32[8,1536]{1,0:T(8,128)S(1)}, f32[8,1536]{1,0:T(8,128)S(1)}, u32[]{:S(2)}, u32[]{:S(2)}) collective-permute-start(f32[8,1536]{1,0:T(8,128)S(1)} %collective-permute-done.2.refs_1_), channel_id=1, source_target_pairs={{0,1},{1,0},{2,3},{3,2},{4,5},{5,4},{6,7},{7,6},{8,9},{9,8},{10,11... | collective-permute-start | bytes 147464 | tf_op jit(solution)/shard_map/ppermute | solution.py:273
